TPU v7x, 256 devices: a whole 4x4x8 slice. The times are simulated.
256 devices in a mesh: cell: 16 (over x, y), sub: 16 (over z, core).
Axes of the slice: x: 4, y: 4, z: 8, core: 2. Of those that a mesh axis runs over, the one named last changes fastest.
Arguments:
- shell_conc: float32 [16, 64, 10, 256, 128], P('cell', 'sub'), may hold values from 0.2 to 0.8
- heat_rise: float32 [16, 30, 256, 128], P('cell', None, 'sub'), may hold values from -5 to 5
- layer_current: float32 [16, 64, 256, 128], P('cell', 'sub'), may hold values from -4 to 4
- layer_counts: int32 [16], replicated, may hold values from 1 to 4, 30 in all
- contacts: int32 [16, 2], replicated, may hold values from -1 to 15, as said below
Outputs:
- conc_new: float32 [16, 64, 10, 256, 128], P('cell', 'sub')
- heat_new: float32 [16, 30, 256, 128], P('cell', None, 'sub')
Inputs may be any that keep to these rules, and one draw needn't show every extreme that they name: `layer_counts`: entry d is the number of consecutive layers held by index d of sub, in order; the entries sum to 30 and the largest is exactly 4. `contacts`: row c names the cell below and the cell above cell c in one stacking order of all 16 cells, each cell once; -1 marks the two ends of the stack.
All inputs are finite; a program needn't handle non-finite values.
Results may differ from a plain program's by a relative error of at most 0.0003.
Values sent between devices are 32-bit elements; how exact they have to be, the bound alone decides.
No kernel may reach another device: no remote copies, remote signals or barrier semaphores. Data moves between devices by JAX's collectives and lax.ppermute only.
A program may use at most 64 MiB of HBM per device.

v0:
```python
import jax
import jax.numpy as jnp
from jax import lax
from jax.sharding import PartitionSpec as P

BASE_KELVIN = 298.15
RATE_ACTIVATION = 5000.0
DIFFUSION_ACTIVATION = 3000.0
RATE_CONSTANT = 0.5
VOLT_PER_KELVIN = 2.0 * 8.314462618 / 96485.33212
HEAT_SCALE = 10.0
ENTROPY_SLOPE = 0.001
DIFFUSION_STEP = 0.005
SURFACE_STEP = 0.005
INPLANE_CONDUCT = 0.25
THROUGH_CONDUCT = 2.0
CONTACT_CONDUCT = 0.5


def with_halo(cells, sides, width):
    for axis, dim in sides:
        count = lax.axis_size(axis)
        ends = count - 1
        head = lax.slice_in_dim(cells, 0, width, axis=dim)
        tail = lax.slice_in_dim(cells, cells.shape[dim] - width, cells.shape[dim], axis=dim)
        cells = jnp.concatenate(
            [
                lax.ppermute(tail, axis, [(i, (i + 1) % count) for i in range(ends)]),
                cells,
                lax.ppermute(head, axis, [((i + 1) % count, i) for i in range(ends)]),
            ],
            axis=dim,
        )
    return cells


def inverse_sine(value):
    magnitude = jnp.abs(value)
    rooted = jnp.sqrt(1.0 + magnitude * magnitude)
    positive = jnp.log1p(magnitude + magnitude * magnitude / (1.0 + rooted))
    return jnp.where(value < 0.0, -positive, positive)


def layer_tables(layer_counts, slot_count, layer_total):
    finish = jnp.cumsum(layer_counts)
    starts = finish - layer_counts
    devices = layer_counts.shape[0]
    device_ids = jnp.arange(devices, dtype=jnp.int32)
    slot_index = jnp.arange(devices * slot_count, dtype=jnp.int32)
    slot_owner = slot_index // slot_count
    slot_place = slot_index % slot_count
    owner_hits = slot_owner[:, None] == device_ids[None, :]
    owner_count = jnp.sum(jnp.where(owner_hits, layer_counts[None, :], 0), axis=1)
    owner_start = jnp.sum(jnp.where(owner_hits, starts[None, :], 0), axis=1)
    live_slot = slot_place < owner_count
    slot_layer = jnp.minimum(owner_start + slot_place, layer_total - 1)
    layer_index = jnp.arange(layer_total, dtype=jnp.int32)
    layer_owner = jnp.sum((finish[None, :] <= layer_index[:, None]).astype(jnp.int32), axis=1)
    layer_hits = layer_owner[:, None] == device_ids[None, :]
    layer_start = jnp.sum(jnp.where(layer_hits, starts[None, :], 0), axis=1)
    layer_slot = layer_owner * slot_count + layer_index - layer_start
    return (live_slot, slot_layer, layer_slot)


def kinetics(surface, kelvin, current):
    reciprocal = 1.0 / BASE_KELVIN - 1.0 / kelvin
    base_rate = (
        RATE_CONSTANT * jnp.exp(RATE_ACTIVATION * reciprocal) * jnp.sqrt(surface * (1.0 - surface))
    )
    ratio_rate = current / (2.0 * base_rate)
    arcsine = inverse_sine(ratio_rate)
    overvoltage = VOLT_PER_KELVIN * kelvin * arcsine
    entropic = ENTROPY_SLOPE * (0.5 - surface)
    source = HEAT_SCALE * current * (overvoltage + kelvin * entropic)
    heat_slope = (
        HEAT_SCALE
        * current
        * (
            VOLT_PER_KELVIN * arcsine
            - VOLT_PER_KELVIN
            * ratio_rate
            * RATE_ACTIVATION
            / (kelvin * jnp.sqrt(1.0 + ratio_rate * ratio_rate))
            + entropic
        )
    )
    return (source, heat_slope)


def particle(states, kelvin, current):
    shells = states.shape[1]
    speedup = jnp.exp(DIFFUSION_ACTIVATION * (1.0 / BASE_KELVIN - 1.0 / kelvin))
    volumes = [((radial + 1) ** 3 - radial**3) / (3.0 * shells**3) for radial in range(shells)]
    linkage = [
        DIFFUSION_STEP * speedup * ((radial + 1) ** 2 / shells**2 * shells)
        for radial in range(shells - 1)
    ]
    uppers = []
    values = []
    for radial in range(shells):
        diagonal = volumes[radial] + jnp.zeros_like(kelvin)
        right_side = volumes[radial] * states[:, radial]
        if radial < shells - 1:
            diagonal = diagonal + linkage[radial]
        else:
            right_side = right_side - SURFACE_STEP * current
        if radial > 0:
            diagonal = diagonal + linkage[radial - 1] - linkage[radial - 1] * uppers[radial - 1]
            right_side = right_side + linkage[radial - 1] * values[radial - 1]
        if radial < shells - 1:
            uppers.append(linkage[radial] / diagonal)
        else:
            uppers.append(jnp.zeros_like(kelvin))
        values.append(right_side / diagonal)
    result = [None] * shells
    result[shells - 1] = values[shells - 1]
    for radial in range(shells - 2, -1, -1):
        result[radial] = values[radial] + uppers[radial] * result[radial + 1]
    return jnp.stack(result, axis=1)


def column_solve(right_side, heat_slope):
    layer_total = right_side.shape[1]
    uppers = []
    values = []
    for height in range(layer_total):
        diagonal = 1.0 - heat_slope[:, height]
        source = right_side[:, height]
        if height > 0:
            diagonal = diagonal + THROUGH_CONDUCT - THROUGH_CONDUCT * uppers[height - 1]
            source = source + THROUGH_CONDUCT * values[height - 1]
        if height < layer_total - 1:
            diagonal = diagonal + THROUGH_CONDUCT
        uppers.append(THROUGH_CONDUCT / diagonal)
        values.append(source / diagonal)
    result = [None] * layer_total
    result[layer_total - 1] = values[layer_total - 1]
    for height in range(layer_total - 2, -1, -1):
        result[height] = values[height] + uppers[height] * result[height + 1]
    return jnp.stack(result, axis=1)


def per_device(shell_conc, heat_rise, layer_current, layer_counts, contacts):
    slot_count = shell_conc.shape[1]
    shells = shell_conc.shape[2]
    layer_total = heat_rise.shape[1]
    live_slot, slot_layer, layer_slot = layer_tables(layer_counts, slot_count, layer_total)
    position = lax.axis_index("sub")
    devices = lax.axis_size("sub")
    outgoing = jnp.take(heat_rise, slot_layer, axis=1)
    slot_rise = lax.all_to_all(outgoing, "sub", split_axis=1, concat_axis=2, tiled=True)
    kelvin = BASE_KELVIN + slot_rise
    surface = shell_conc[:, :, shells - 1]
    source, heat_slope = kinetics(surface, kelvin, layer_current)
    got_source, got_slope = (
        lax.all_to_all(source, "sub", split_axis=2, concat_axis=1, tiled=True),
        lax.all_to_all(heat_slope, "sub", split_axis=2, concat_axis=1, tiled=True),
    )
    layer_source = jnp.take(got_source, layer_slot, axis=1)
    layer_slope = jnp.take(got_slope, layer_slot, axis=1)
    updated = particle(shell_conc[0], kelvin[0], layer_current[0])[None]
    own_live = lax.dynamic_slice_in_dim(live_slot, position * slot_count, slot_count)
    conc_new = jnp.where(own_live[None, :, None, None, None], updated, 0.0)
    face_rows = jnp.stack([heat_rise[:, 0], heat_rise[:, layer_total - 1]], axis=1)
    every_face = lax.all_gather(face_rows, "cell", axis=0, tiled=True)
    partners = lax.dynamic_index_in_dim(contacts, lax.axis_index("cell"), 0, keepdims=False)
    lower_pair = lax.dynamic_index_in_dim(
        every_face, jnp.maximum(partners[0], 0), 0, keepdims=False
    )
    upper_pair = lax.dynamic_index_in_dim(
        every_face, jnp.maximum(partners[1], 0), 0, keepdims=False
    )
    below_face = jnp.where(partners[0] >= 0, lower_pair[1], 0.0)[None]
    above_face = jnp.where(partners[1] >= 0, upper_pair[0], 0.0)[None]
    rim_rows = with_halo(heat_rise, (("sub", 2),), 1)
    low_row = jnp.where(position == 0, heat_rise[:, :, 0:1], rim_rows[:, :, 0:1])
    high_row = jnp.where(position == devices - 1, heat_rise[:, :, -1:], rim_rows[:, :, -1:])
    column_pad = jnp.concatenate([low_row, heat_rise, high_row], axis=2)
    row_pad = jnp.pad(heat_rise, ((0, 0), (0, 0), (0, 0), (1, 1)), mode="edge")
    laplace = (
        column_pad[:, :, 2:]
        + column_pad[:, :, :-2]
        + row_pad[:, :, :, 2:]
        + row_pad[:, :, :, :-2]
        - 4.0 * heat_rise
    )
    right_side = heat_rise + INPLANE_CONDUCT * laplace + layer_source - layer_slope * heat_rise
    first_row = right_side[:, 0] + CONTACT_CONDUCT * (below_face - heat_rise[:, 0])
    last_row = right_side[:, layer_total - 1] + CONTACT_CONDUCT * (
        above_face - heat_rise[:, layer_total - 1]
    )
    right_side = jnp.concatenate(
        [first_row[:, None], right_side[:, 1 : layer_total - 1], last_row[:, None]], axis=1
    )
    heat_new = column_solve(right_side, layer_slope)
    return (conc_new, heat_new)


def solution(mesh):
    in_specs = (
        P("cell", "sub", None, None, None),
        P("cell", None, "sub", None),
        P("cell", "sub", None, None),
        P(),
        P(),
    )
    out_specs = (P("cell", "sub", None, None, None), P("cell", None, "sub", None))
    return jax.shard_map(
        per_device, mesh=mesh, in_specs=in_specs, out_specs=out_specs, check_vma=False
    )
```

profile of v0, /device:TPU:1, one launch (start us, length us, event | category | flops | bytes accessed | tf_op | source)
XLA Modules:
  0.0 119.1 jit_solution(16911137274033418528)
XLA Ops:
  0.6 1.0 fusion.193
  1.6 5.1 %collective-permute-start = (f32[1,30,1,128]{3,2,1,0:T(1,128)S(1)}, f32[1,30,1,128]{3,2,1,0:T(1,128)S(1)}, u32[]{:S(2)}, u32[]{:S(2)}) collective-permute-start(f32[1,30,1,128]{3,2,1,0:T(1,128)S(1)} %get-tuple-element.86), channel_id=1, source_target_pairs={{1,0},{2,1},{3,2},{4,3},{5,4},{6,5},{7,6},{8,7},{9,8},{10,9},{11,1... | collective-permute-start | bytes 46088 | tf_op jit(solution)/shard_map/ppermute | solution.py:30
  6.8 1.9 %collective-permute-start.1 = (f32[1,30,1,128]{3,2,1,0:T(1,128)S(1)}, f32[1,30,1,128]{3,2,1,0:T(1,128)S(1)}, u32[]{:S(2)}, u32[]{:S(2)}) collective-permute-start(f32[1,30,1,128]{3,2,1,0:T(1,128)S(1)} %get-tuple-element.87), channel_id=1, source_target_pairs={{0,1},{1,2},{2,3},{3,4},{4,5},{5,6},{6,7},{7,8},{8,9},{9,10},{10,1... | collective-permute-start | bytes 46088 | tf_op jit(solution)/shard_map/ppermute | solution.py:28
  8.7 0.7 copy.132
  9.5 0.1 reduce
  9.6 0.7 sub.2586
  10.3 0.7 select_reduce_fusion.2
  11.1 1.5 %gather_fusion = f32[64,16,128]{2,1,0:T(8,128)S(1)} fusion(f32[30,16,128]{2,1,0:T(8,128)} %bitcast.443, s32[1024]{0:T(1024)S(1)} %pad_clamp_fusion.1), kind=kCustom, calls=%fused_computation.2 | custom fusion | bytes 1048832 | tf_op jit(solution)/shard_map/jit(_take)/gather | solution.py:150
  12.6 0.9 bitcast_select_fusion
  13.5 7.9 %all-to-all-start = ((f32[1,64,16,128]{3,2,0,1:T(8,128)}), f32[1,64,16,128]{3,2,0,1:T(8,128)S(1)}, u32[]{:S(2)}, u32[]{:S(2)}) async-start(f32[1,64,16,128]{3,2,0,1:T(8,128)} %bitcast_select_fusion), calls=%async_computation | async-start | bytes 1048576 | tf_op jit(solution)/shard_map/all_to_all | solution.py:151
  21.5 0.1 convert_reduce_fusion
  21.5 0.7 fusion.195
  22.3 0.1 select_reduce_fusion
  22.4 0.1 constant_dynamic-slice_fusion
  22.5 0.5 fusion.196
  23.0 1.9 %fusion.194 = (f32[1,30,16,1]{3,2,1,0:T(8,128)}, f32[1,30,16,1]{3,2,1,0:T(8,128)}) fusion(f32[1,30,16,128]{3,2,1,0:T(8,128)} %param.8), kind=kLoop, calls=%fused_computation.427 | loop fusion | bytes 7680 | tf_op jit(solution)/shard_map/jit(_pad)/slice | solution.py:179
  24.9 21.1 %all_gather.3 = f32[16,2,16,128]{3,2,1,0:T(8,128)} all-gather(f32[1,2,16,128]{3,2,1,0:T(8,128)S(1)} %pad_maximum_fusion.4), channel_id=1, replica_groups=mesh['cell'=16,'sub'=16] {'cell'}, dimensions={0}, use_global_device_ids=true | all-gather | bytes 278528 | tf_op jit(solution)/shard_map/all_gather | solution.py:165
  48.4 5.5 %copy.161 = f32[1,4,10,256,128]{4,3,1,2,0:T(8,128)} copy(f32[1,4,10,256,128]{4,3,2,1,0:T(8,128)} %param.7) | data formatting | bytes 10485760 | tf_op args[0]
  54.1 0.5 broadcast_add_fusion
  55.0 0.9 copy.139
  55.8 0.9 copy.140
  56.7 0.9 copy.141
  57.6 2.9 %fusion.33 = (f32[1,4,256,128]{3,2,1,0:T(8,128)S(1)}, f32[1,4,256,128]{3,2,1,0:T(8,128)}) fusion(f32[1,16,4,16,128]{4,3,1,2,0:T(8,128)S(1)} %copy.151, f32[1,4,256,128]{3,2,1,0:T(8,128)S(1)} %copy-done.5, f32[1,4,10,256,128]{4,3,1,2,0:T(8,128)} %copy.161), kind=kLoop, calls=%fused_computation.65 | loop fusion | flops 4325376 | bytes 2621440 | tf_op jit(solution)/shard_map/mul | solution.py:76
  60.5 1.2 copy.156
  61.7 12.0 %all-to-all-start.2 = ((f32[1,4,256,128]{3,1,0,2:T(4,128)}), f32[1,4,256,128]{3,1,0,2:T(4,128)}, u32[]{:S(2)}, u32[]{:S(2)}) async-start(f32[1,4,256,128]{3,1,0,2:T(4,128)} %copy.156), calls=%async_computation.2 | async-start | bytes 1048576 | tf_op jit(solution)/shard_map/all_to_all | solution.py:157
  73.7 2.2 %copy.153 = f32[1,4,256,128]{3,1,0,2:T(4,128)} copy(f32[1,4,256,128]{3,2,1,0:T(8,128)} %get-tuple-element.67) | data formatting | bytes 1048576 | tf_op jit(solution)/shard_map/mul | solution.py:74
  75.9 3.9 %fusion.10 = (f32[4,1,256,128]{3,2,0,1:T(8,128)S(1)}, f32[4,1,256,128]{3,2,0,1:T(8,128)S(1)}, f32[4,1,256,128]{3,2,0,1:T(8,128)S(1)}, f32[4,1,256,128]{3,2,0,1:T...) fusion(f32[4,10,256,128]{3,2,0,1:T(8,128)} %bitcast.441, ...), kind=kLoop, calls=%fused_computation.22 | loop fusion | flops 8650752 | bytes 14155776 | tf_op jit(solution)/shard_map/div | solution.py:114
  79.8 4.1 %multiply_add_fusion.1 = (f32[4,1,256,128]{3,2,0,1:T(8,128)S(1)}, f32[4,1,256,128]{3,2,0,1:T(8,128)S(1)}, f32[4,1,256,128]{3,2,0,1:T(8,128)S(1)}, f32[4,1,256,12...) fusion(f32[4,1,256,128]{3,2,0,1:T(8,128)S(1)} %get-tuple-element.65,, ...), kind=kLoop, calls=%fused_computation.124 | loop fusion | flops 8126464 | bytes 15728640 | tf_op jit(solution)/shard_map/add | solution.py:118
  83.9 0.9 bitcast_dynamic-update-slice_fusion.8
  84.8 0.8 bitcast_dynamic-update-slice_fusion.7
  85.6 0.9 bitcast_dynamic-update-slice_fusion.6
  86.5 0.8 bitcast_dynamic-update-slice_fusion.5
  87.3 0.9 bitcast_dynamic-update-slice_fusion.4
  88.2 0.8 bitcast_dynamic-update-slice_fusion.3
  89.0 0.9 bitcast_dynamic-update-slice_fusion.2
  89.8 0.8 bitcast_dynamic-update-slice_fusion.1
  90.7 0.4 all-to-all-done.2
  91.1 6.8 %all-to-all-start.1 = ((f32[1,4,256,128]{3,1,0,2:T(4,128)}), f32[1,4,256,128]{3,1,0,2:T(4,128)S(1)}, u32[]{:S(2)}, u32[]{:S(2)}) async-start(f32[1,4,256,128]{3,1,0,2:T(4,128)} %copy.153), calls=%async_computation.1 | async-start | bytes 1048576 | tf_op jit(solution)/shard_map/all_to_all | solution.py:156
  97.9 0.9 bitcast_dynamic-update-slice_fusion
  98.8 0.8 bitcast_dynamic-update-slice_fusion.9
  99.6 5.7 %broadcast_select_fusion = f32[1,4,10,256,128]{4,3,2,1,0:T(8,128)} fusion(f32[1,4,10,256,128]{4,3,2,1,0:T(8,128)} %bitcast_dynamic-update-slice_fusion.9, pred[4]{0:T(512)(128)(4,1)S(1)} %dynamic_slice.14), kind=kLoop, calls=%fused_computation.3 | loop fusion | flops 1310720 | bytes 10485764 | tf_op jit(solution)/shard_map/jit(_where)/select_n | solution.py:163
  105.3 1.1 copy.157
  106.5 8.8 %all-to-all-done.1 = f32[1,4,256,128]{3,1,0,2:T(4,128)S(1)} async-done(((f32[1,4,256,128]{3,1,0,2:T(4,128)}), f32[1,4,256,128]{3,1,0,2:T(4,128)S(1)}, u32[]{:S(2)}, u32[]{:S(2)}) %all-to-all-start.1) | async-done | bytes 524320 | tf_op jit(solution)/shard_map/all_to_all | solution.py:156
  115.3 0.6 gather_fusion.2
  115.9 0.6 gather_fusion.1
  116.5 0.3 bitcast_select_fusion.1
  116.9 1.2 constant_dynamic-update-slice_fusion.29
  118.4 0.7 copy-done.12
  (78 shorter events, 0.9 us)
Async XLA Ops:
  0.6 21.7 %copy-start = (s32[16,2]{0,1:T(2,128)S(1)}, s32[16,2]{0,1:T(2,128)}, u32[]{:S(2)}) copy-start(s32[16,2]{0,1:T(2,128)} %param.11) | copy-start | bytes 388
  1.6 52.4 %collective-permute-start = (f32[1,30,1,128]{3,2,1,0:T(1,128)S(1)}, f32[1,30,1,128]{3,2,1,0:T(1,128)S(1)}, u32[]{:S(2)}, u32[]{:S(2)}) collective-permute-start(f32[1,30,1,128]{3,2,1,0:T(1,128)S(1)} %get-tuple-element.86), channel_id=1, source_target_pairs={{1,0},{2,1},{3,2},{4,3},{5,4},{6,5},{7,6},{8,7},{9,8},{10,9},{11,1... | collective-permute-start | bytes 46088 | tf_op jit(solution)/shard_map/ppermute | solution.py:30
  6.8 47.2 %collective-permute-start.1 = (f32[1,30,1,128]{3,2,1,0:T(1,128)S(1)}, f32[1,30,1,128]{3,2,1,0:T(1,128)S(1)}, u32[]{:S(2)}, u32[]{:S(2)}) collective-permute-start(f32[1,30,1,128]{3,2,1,0:T(1,128)S(1)} %get-tuple-element.87), channel_id=1, source_target_pairs={{0,1},{1,2},{2,3},{3,4},{4,5},{5,6},{6,7},{7,8},{8,9},{9,10},{10,1... | collective-permute-start | bytes 46088 | tf_op jit(solution)/shard_map/ppermute | solution.py:28
  13.5 40.5 %all-to-all-start = ((f32[1,64,16,128]{3,2,0,1:T(8,128)}), f32[1,64,16,128]{3,2,0,1:T(8,128)S(1)}, u32[]{:S(2)}, u32[]{:S(2)}) async-start(f32[1,64,16,128]{3,2,0,1:T(8,128)} %bitcast_select_fusion), calls=%async_computation | async-start | bytes 1048576 | tf_op jit(solution)/shard_map/all_to_all | solution.py:151
  48.4 5.6 %copy-start.1 = (f32[1,30,16,128]{3,2,1,0:T(8,128)S(1)}, f32[1,30,16,128]{3,2,1,0:T(8,128)}, u32[]{:S(2)}) copy-start(f32[1,30,16,128]{3,2,1,0:T(8,128)} %param.8) | copy-start | bytes 737284
  54.6 2.9 %copy-start.5 = (f32[1,4,256,128]{3,2,1,0:T(8,128)S(1)}, f32[1,4,256,128]{3,2,1,0:T(8,128)}, u32[]{:S(2)}) copy-start(f32[1,4,256,128]{3,2,1,0:T(8,128)} %param.9) | copy-start | bytes 1572868
  61.7 29.4 %all-to-all-start.2 = ((f32[1,4,256,128]{3,1,0,2:T(4,128)}), f32[1,4,256,128]{3,1,0,2:T(4,128)}, u32[]{:S(2)}, u32[]{:S(2)}) async-start(f32[1,4,256,128]{3,1,0,2:T(4,128)} %copy.156), calls=%async_computation.2 | async-start | bytes 1048576 | tf_op jit(solution)/shard_map/all_to_all | solution.py:157
  75.9 3.9 %copy-start.2 = (f32[1,4,16,16,128]{4,3,2,1,0:T(8,128)S(1)}, f32[1,4,16,16,128]{4,3,2,1,0:T(8,128)}, u32[]{:S(2)}) copy-start(f32[1,4,16,16,128]{4,3,2,1,0:T(8,128)} %copy.139) | copy-start | bytes 1572868
  75.9 3.9 %copy-start.3 = (f32[1,4,16,16,128]{4,3,2,1,0:T(8,128)S(1)}, f32[1,4,16,16,128]{4,3,2,1,0:T(8,128)}, u32[]{:S(2)}) copy-start(f32[1,4,16,16,128]{4,3,2,1,0:T(8,128)} %copy.140) | copy-start | bytes 1572868
  75.9 3.9 %copy-start.6 = (f32[1,4,256,128]{3,2,1,0:T(8,128)S(1)}, f32[1,4,256,128]{3,2,1,0:T(8,128)}, u32[]{:S(2)}) copy-start(f32[1,4,256,128]{3,2,1,0:T(8,128)} %param.9) | copy-start | bytes 1572868
  75.9 3.9 %copy-start.7 = (f32[1,4,16,16,128]{4,3,2,1,0:T(8,128)S(1)}, f32[1,4,16,16,128]{4,3,2,1,0:T(8,128)}, u32[]{:S(2)}) copy-start(f32[1,4,16,16,128]{4,3,2,1,0:T(8,128)} %copy.141) | copy-start | bytes 1572868
  85.6 12.3 %copy-start.4 = (f32[4,1,256,128]{3,2,0,1:T(8,128)S(1)}, f32[4,1,256,128]{3,2,0,1:T(8,128)}, u32[]{:S(2)}) copy-start(f32[4,1,256,128]{3,2,0,1:T(8,128)} %get-tuple-element.54) | copy-start | bytes 1572868
  85.6 12.3 %copy-start.8 = (f32[4,1,256,128]{3,2,0,1:T(8,128)S(1)}, f32[4,1,256,128]{3,2,0,1:T(8,128)}, u32[]{:S(2)}) copy-start(f32[4,1,256,128]{3,2,0,1:T(8,128)} %get-tuple-element.55) | copy-start | bytes 1572868
  85.6 12.3 %copy-start.9 = (f32[4,1,256,128]{3,2,0,1:T(8,128)S(1)}, f32[4,1,256,128]{3,2,0,1:T(8,128)}, u32[]{:S(2)}) copy-start(f32[4,1,256,128]{3,2,0,1:T(8,128)} %get-tuple-element.56) | copy-start | bytes 1572868
  91.1 24.1 %all-to-all-start.1 = ((f32[1,4,256,128]{3,1,0,2:T(4,128)}), f32[1,4,256,128]{3,1,0,2:T(4,128)S(1)}, u32[]{:S(2)}, u32[]{:S(2)}) async-start(f32[1,4,256,128]{3,1,0,2:T(4,128)} %copy.153), calls=%async_computation.1 | async-start | bytes 1048576 | tf_op jit(solution)/shard_map/all_to_all | solution.py:156
  99.6 16.9 %copy-start.10 = (f32[1,30,16,1]{3,2,1,0:T(8,128)S(1)}, f32[1,30,16,1]{3,2,1,0:T(8,128)}, u32[]{:S(2)}) copy-start(f32[1,30,16,1]{3,2,1,0:T(8,128)} %get-tuple-element.88) | copy-start | bytes 5764
  99.6 16.9 %copy-start.11 = (f32[1,30,16,1]{3,2,1,0:T(8,128)S(1)}, f32[1,30,16,1]{3,2,1,0:T(8,128)}, u32[]{:S(2)}) copy-start(f32[1,30,16,1]{3,2,1,0:T(8,128)} %get-tuple-element.89) | copy-start | bytes 5764
  118.4 0.7 copy-start.12
where the time goes:
time: 120 us; the launch traced here: 119 us
  starting transfers between devices  33.8 us (28%)
  other arithmetic  25.8 us (22%)
  local copies, waits for them, and re-layouts  25.6 us (21%)
  blocking collectives  21.1 us (18%)
  waiting for transfers between devices  9.19 us (8%)
  between operations  3.58 us (3%)
    all_gather x1, blocking collectives, per_device(): every_face = lax.all_gather(face_rows, 'cell', axis=0, tiled=True)  21.1 us
    all_to_all x1, starting transfers between devices, per_device(): lax.all_to_all(heat_slope, 'sub', split_axis=2, concat_axis=1, tiled=True)  12 us
    unnamed x46, local copies, waits for them, and re-layouts  9.59 us
    all_to_all x1, waiting for transfers between devices, per_device(): lax.all_to_all(source, 'sub', split_axis=2, concat_axis=1, tiled=True)  8.76 us
    all_to_all x1, starting transfers between devices, per_device(): lax.all_to_all(outgoing, 'sub', split_axis=1, concat_axis=2, tiled=True)  7.91 us
    all_to_all x1, starting transfers between devices, per_device(): lax.all_to_all(source, 'sub', split_axis=2, concat_axis=1, tiled=True)  6.8 us
    select_n x1, other arithmetic, per_device(): conc_new = jnp.where(own_live[None, :, None, None, None], updated, 0.0)  5.69 us
    unnamed x19, other arithmetic  5.63 us
  transfers between devices with their start and end apart: 5, of which 2 were waited for; matrix products, arithmetic and copies ran while one was open for 33% of the time, Pallas kernels for 0%

commit v1 on v0

v1 whole, which is shorter than its diff:
```python
import functools

import jax
import jax.numpy as jnp
from jax import lax
from jax.experimental import pallas as pl
from jax.experimental.pallas import tpu as pltpu
from jax.sharding import PartitionSpec as P

BASE_KELVIN = 298.15
RATE_ACTIVATION = 5000.0
DIFFUSION_ACTIVATION = 3000.0
RATE_CONSTANT = 0.5
VOLT_PER_KELVIN = 2.0 * 8.314462618 / 96485.33212
HEAT_SCALE = 10.0
ENTROPY_SLOPE = 0.001
DIFFUSION_STEP = 0.005
SURFACE_STEP = 0.005
INPLANE_CONDUCT = 0.25
THROUGH_CONDUCT = 2.0
CONTACT_CONDUCT = 0.5

SMEM = pltpu.MemorySpace.SMEM
VMEM = pltpu.MemorySpace.VMEM


def reciprocal(value):
    guess = pl.reciprocal(value, approx=True)
    return guess * (2.0 - value * guess)


def starts_of(counts_ref, devices):
    starts = [jnp.int32(0)]
    for d in range(devices):
        starts.append(starts[-1] + counts_ref[d])
    return starts


def pack_rise(heat_rise, layer_counts, slots):
    layers, rows, columns = heat_rise.shape
    devices = layer_counts.shape[0]

    def kernel(counts_ref, heat_ref, send_ref, low_ref, high_ref):
        starts = starts_of(counts_ref, devices)
        for d in range(devices):
            for s in range(slots):
                layer = jnp.minimum(starts[d] + s, layers - 1)
                send_ref[d * slots + s] = heat_ref[layer]
        for layer in range(layers):
            low_ref[layer : layer + 1] = heat_ref[layer, 0:1]
            high_ref[layer : layer + 1] = heat_ref[layer, rows - 1 : rows]

    edge = jax.ShapeDtypeStruct((layers, columns), jnp.float32)
    return pl.pallas_call(
        kernel,
        name="pack_rise",
        out_shape=(
            jax.ShapeDtypeStruct((devices * slots, rows, columns), jnp.float32),
            edge,
            edge,
        ),
        in_specs=[pl.BlockSpec(memory_space=SMEM), pl.BlockSpec(memory_space=VMEM)],
        out_specs=[pl.BlockSpec(memory_space=VMEM)] * 3,
    )(layer_counts, heat_rise)


def pack_kinetic(shell_conc, layer_current, devices):
    slots, shells, rows, columns = shell_conc.shape
    part = rows // devices

    def kernel(shell_ref, current_ref, send_ref, sem):
        copies = []
        for d in range(devices):
            here = pl.ds(d * part, part)
            copies.append(
                pltpu.make_async_copy(shell_ref.at[:, shells - 1, here], send_ref.at[d, 0], sem.at[2 * d])
            )
            copies.append(
                pltpu.make_async_copy(current_ref.at[:, here], send_ref.at[d, 1], sem.at[2 * d + 1])
            )
        for copy in copies:
            copy.start()
        for copy in copies:
            copy.wait()

    return pl.pallas_call(
        kernel,
        name="pack_kinetic",
        out_shape=jax.ShapeDtypeStruct((devices, 2, slots, part, columns), jnp.float32),
        in_specs=[pl.BlockSpec(memory_space=pl.ANY)] * 2,
        out_specs=pl.BlockSpec(memory_space=VMEM),
        scratch_shapes=[pltpu.SemaphoreType.DMA((2 * devices,))],
    )(shell_conc, layer_current)


def particle(shell_conc, slot_rise, layer_current, layer_counts, chunk=32):
    slots, shells, rows, columns = shell_conc.shape
    sources, _, part, _ = slot_rise.shape
    halves = 2
    block = rows // halves
    volume = [((i + 1) ** 3 - i**3) / (3.0 * shells**3) for i in range(shells)]
    link = [DIFFUSION_STEP * ((i + 1) ** 2 / shells**2 * shells) for i in range(shells - 1)]

    def kernel(counts_ref, shell_ref, rise_ref, current_ref, out_ref):
        live = pl.program_id(0) < counts_ref[lax.axis_index("sub")]

        @pl.when(jnp.logical_not(live))
        def _():
            out_ref[...] = jnp.zeros_like(out_ref)

        @pl.when(live)
        def _():
            for c in range(block // chunk):
                here = slice(c * chunk, (c + 1) * chunk)
                rise = jnp.concatenate(
                    [rise_ref[c * chunk // part + k, 0] for k in range(chunk // part)], axis=0
                )
                scaled = rise * (DIFFUSION_ACTIVATION / BASE_KELVIN)
                speedup = jnp.exp(scaled * reciprocal(BASE_KELVIN + rise))
                held = [None] * shells
                inverse = [None] * shells
                capacity = amount = None
                for i in range(shells):
                    gain = volume[i] * shell_ref[0, i, here]
                    if i == 0:
                        capacity, amount = volume[0], gain
                    else:
                        capacity = volume[i] + upper * capacity
                        amount = gain + upper * amount
                    if i < shells - 1:
                        flow = link[i] * speedup
                        inverse[i] = reciprocal(capacity + flow)
                        upper = flow * inverse[i]
                    else:
                        amount = amount - SURFACE_STEP * current_ref[0, here]
                        inverse[i] = reciprocal(capacity)
                    held[i] = amount
                value = held[-1] * inverse[-1]
                out_ref[0, shells - 1, here] = value
                for i in range(shells - 2, -1, -1):
                    value = inverse[i] * (held[i] + (link[i] * speedup) * value)
                    out_ref[0, i, here] = value

    return pl.pallas_call(
        kernel,
        name="particle",
        grid=(slots, halves),
        out_shape=jax.ShapeDtypeStruct(shell_conc.shape, jnp.float32),
        in_specs=[
            pl.BlockSpec(memory_space=SMEM),
            pl.BlockSpec((1, shells, block, columns), lambda s, h: (s, 0, h, 0)),
            pl.BlockSpec((sources // halves, 1, part, columns), lambda s, h: (h, s, 0, 0)),
            pl.BlockSpec((1, block, columns), lambda s, h: (s, h, 0)),
        ],
        out_specs=pl.BlockSpec((1, shells, block, columns), lambda s, h: (s, 0, h, 0)),
        cost_estimate=pl.CostEstimate(
            flops=20 * slots * shells * rows * columns,
            bytes_accessed=8 * slots * shells * rows * columns,
            transcendentals=0,
        ),
    )(layer_counts, shell_conc, slot_rise, layer_current)


def inverse_sine(value):
    magnitude = jnp.abs(value)
    rooted = jnp.sqrt(1.0 + magnitude * magnitude)
    positive = jnp.log1p(magnitude + magnitude * magnitude / (1.0 + rooted))
    return jnp.where(value < 0.0, -positive, positive), rooted


def column(heat_rise, kinetic, low, high, faces, layer_counts, contacts):
    layers, rows, columns = heat_rise.shape
    devices = layer_counts.shape[0]
    slots = kinetic.shape[0] // (2 * devices)
    last = layers - 1

    def kernel(counts_ref, contacts_ref, heat_ref, kinetic_ref, low_ref, high_ref, faces_ref, out_ref, place, slope_ref, right_ref):
        position = lax.axis_index("sub")
        cell = lax.axis_index("cell")
        starts = starts_of(counts_ref, devices)
        for d in range(devices):
            for s in range(slots):
                place[starts[d] + s] = 2 * slots * d + s
        row_id = lax.broadcasted_iota(jnp.int32, (rows, columns), 0)
        lane_id = lax.broadcasted_iota(jnp.int32, (rows, columns), 1)
        for layer in range(layers):
            rise = heat_ref[layer]
            low_row = jnp.where(position == 0, rise[0:1], low_ref[layer : layer + 1])
            high_row = jnp.where(position == devices - 1, rise[rows - 1 : rows], high_ref[layer : layer + 1])
            laplace = (
                jnp.where(row_id == 0, low_row, pltpu.roll(rise, 1, 0))
                + jnp.where(row_id == rows - 1, high_row, pltpu.roll(rise, rows - 1, 0))
                + jnp.where(lane_id == 0, rise, pltpu.roll(rise, 1, 1))
                + jnp.where(lane_id == columns - 1, rise, pltpu.roll(rise, columns - 1, 1))
                - 4.0 * rise
            )
            where = place[layer]
            surface = kinetic_ref[where]
            current = kinetic_ref[where + slots]
            kelvin = BASE_KELVIN + rise
            inverse_kelvin = 1.0 / kelvin
            base_rate = (
                RATE_CONSTANT
                * jnp.exp((RATE_ACTIVATION / BASE_KELVIN) * rise * inverse_kelvin)
                * jnp.sqrt(surface * (1.0 - surface))
            )
            ratio_rate = current / (2.0 * base_rate)
            arcsine, rooted = inverse_sine(ratio_rate)
            entropic = ENTROPY_SLOPE * (0.5 - surface)
            drive = VOLT_PER_KELVIN * arcsine + entropic
            scaled = HEAT_SCALE * current
            source = scaled * (kelvin * drive)
            slope = scaled * (
                drive - (VOLT_PER_KELVIN * RATE_ACTIVATION) * ratio_rate * inverse_kelvin / rooted
            )
            right = rise + INPLANE_CONDUCT * laplace + source - slope * rise
            if layer == 0 or layer == last:
                side = 0 if layer == 0 else 1
                partner = contacts_ref[cell, side]
                face = faces_ref[jnp.maximum(partner, 0) ^ cell, 1 - side]
                face = jnp.where(partner >= 0, face, 0.0)
                right = right + CONTACT_CONDUCT * (face - rise)
            slope_ref[layer] = slope
            right_ref[layer] = right
        upper = value = None
        for layer in range(layers):
            diagonal = 1.0 - slope_ref[layer]
            source = right_ref[layer]
            if layer > 0:
                diagonal = diagonal + THROUGH_CONDUCT - THROUGH_CONDUCT * upper
                source = source + THROUGH_CONDUCT * value
            if layer < last:
                diagonal = diagonal + THROUGH_CONDUCT
            inverse = 1.0 / diagonal
            upper = THROUGH_CONDUCT * inverse
            value = source * inverse
            slope_ref[layer] = upper
            right_ref[layer] = value
        out_ref[last] = value
        for layer in range(last - 1, -1, -1):
            value = right_ref[layer] + slope_ref[layer] * value
            out_ref[layer] = value

    return pl.pallas_call(
        kernel,
        name="column",
        out_shape=jax.ShapeDtypeStruct(heat_rise.shape, jnp.float32),
        in_specs=[pl.BlockSpec(memory_space=SMEM)] * 2 + [pl.BlockSpec(memory_space=VMEM)] * 5,
        out_specs=pl.BlockSpec(memory_space=VMEM),
        scratch_shapes=[
            pltpu.SMEM((layers + slots,), jnp.int32),
            pltpu.VMEM((layers, rows, columns), jnp.float32),
            pltpu.VMEM((layers, rows, columns), jnp.float32),
        ],
        cost_estimate=pl.CostEstimate(
            flops=200 * layers * rows * columns, bytes_accessed=8 * layers * rows * columns, transcendentals=0
        ),
    )(layer_counts, contacts, heat_rise, kinetic, low, high, faces)


def per_device(shell_conc, heat_rise, layer_current, layer_counts, contacts):
    shell_conc, heat_rise, layer_current = shell_conc[0], heat_rise[0], layer_current[0]
    slots = shell_conc.shape[0]
    layers, part, columns = heat_rise.shape
    devices = lax.axis_size("sub")
    cells = lax.axis_size("cell")
    send_rise, low_edge, high_edge = pack_rise(heat_rise, layer_counts, slots)
    send_kinetic = pack_kinetic(shell_conc, layer_current, devices)
    got_rise = lax.all_to_all(send_rise.reshape(devices, slots, part, columns), "sub", 0, 0)
    got_kinetic = lax.all_to_all(send_kinetic, "sub", 0, 0)
    low = lax.ppermute(high_edge, "sub", [(i, i + 1) for i in range(devices - 1)])
    high = lax.ppermute(low_edge, "sub", [(i + 1, i) for i in range(devices - 1)])
    faces = jnp.stack([heat_rise[0], heat_rise[layers - 1]])[None]
    step = 1
    while step < cells:
        other = lax.ppermute(faces, "cell", [(i, i ^ step) for i in range(cells)])
        faces = jnp.concatenate([faces, other], axis=0)
        step *= 2
    conc_new = particle(shell_conc, got_rise, layer_current, layer_counts)
    heat_new = column(
        heat_rise, got_kinetic.reshape(-1, part, columns), low, high, faces, layer_counts, contacts
    )
    return conc_new[None], heat_new[None]


def solution(mesh):
    in_specs = (
        P("cell", "sub", None, None, None),
        P("cell", None, "sub", None),
        P("cell", "sub", None, None),
        P(),
        P(),
    )
    out_specs = (P("cell", "sub", None, None, None), P("cell", None, "sub", None))
    return jax.shard_map(
        per_device, mesh=mesh, in_specs=in_specs, out_specs=out_specs, check_vma=False
    )
```

time: 120 us -> 68.8 us (0.57)
  the two profiles are of different devices: /device:TPU:1 before, /device:TPU:132 now
where the time goes in v1:
time: 68.8 us; the launch traced here: 67.7 us
  starting transfers between devices  27.2 us (40%)
  waiting for transfers between devices  22.6 us (33%)
  Pallas kernels  14.7 us (21%)
  local copies, waits for them, and re-layouts  2.41 us (4%)
  between operations  0.79 us (1%)
    ppermute x4, waiting for transfers between devices, per_device(): other = lax.ppermute(faces, 'cell', [(i, i ^ step) for i in range(cells)])  12 us
    all_to_all x1, waiting for transfers between devices, per_device(): lax.all_to_all(send_rise.reshape(devices, slots, part, columns), 'sub', 0...  10.6 us
    pallas_call x1, Pallas kernels, particle(): pl.pallas_call(kernel, name='particle', grid=(slots, halves), out_shape=j...  7.47 us
    all_to_all x1, starting transfers between devices, per_device(): lax.all_to_all(send_rise.reshape(devices, slots, part, columns), 'sub', 0...  7.36 us
    all_to_all x1, starting transfers between devices, per_device(): got_kinetic = lax.all_to_all(send_kinetic, 'sub', 0, 0)  7.23 us
    ppermute x4, starting transfers between devices, per_device(): other = lax.ppermute(faces, 'cell', [(i, i ^ step) for i in range(cells)])  5.85 us
    ppermute x1, starting transfers between devices, per_device(): lax.ppermute(low_edge, 'sub', [(i + 1, i) for i in range(devices - 1)])  4.85 us
    pallas_call x1, Pallas kernels, column(): pl.pallas_call(kernel, name='column', out_shape=jax.ShapeDtypeStruct(heat...  2.97 us
  transfers between devices with their start and end apart: 8, of which 4 were waited for; matrix products, arithmetic and copies ran while one was open for 2% of the time, Pallas kernels for 15%

profile of v1, /device:TPU:132, one launch (start us, length us, event | category | flops | bytes accessed | tf_op | source)
XLA Modules:
  0.0 67.7 jit_solution(15742418971892729339)
XLA Ops:
  0.6 0.0 copy-start.5
  0.6 1.9 %pack_rise.1 = (f32[64,16,128]{2,1,0:T(8,128)}, f32[30,128]{1,0:T(8,128)}, f32[30,128]{1,0:T(8,128)}) custom-call(s32[16]{0:T(128)} %counts_ref.5, f32[30,16,128]{2,1,0:T(8,128)} %bitcast.21), custom_call_target="tpu_custom_call" | custom-call | tf_op jit(solution)/shard_map/pack_rise/pallas_call | solution.py:54
  2.5 0.0 copy-start.7
  2.5 0.0 copy-start.6
  2.5 7.4 %all-to-all-start = ((f32[16,4,16,128]{3,2,1,0:T(8,128)}), f32[16,4,16,128]{3,2,1,0:T(8,128)S(1)}, u32[]{:S(2)}, u32[]{:S(2)}) async-start(f32[16,4,16,128]{3,2,1,0:T(8,128)} %bitcast.23), calls=%async_computation | async-start | bytes 1048576 | tf_op jit(solution)/shard_map/all_to_all | solution.py:269
  9.9 2.4 %pack_kinetic.1 = f32[16,2,4,16,128]{4,3,2,1,0:T(8,128)} custom-call(f32[4,10,256,128]{3,2,1,0:T(8,128)} %bitcast.15, f32[4,256,128]{2,1,0:T(8,128)} %bitcast.19), custom_call_target="tpu_custom_call" | custom-call | tf_op jit(solution)/shard_map/pack_kinetic/pallas_call | solution.py:86
  12.3 10.6 %all-to-all-done.rise_ref = f32[16,4,16,128]{3,2,1,0:T(8,128)S(1)} async-done(((f32[16,4,16,128]{3,2,1,0:T(8,128)}), f32[16,4,16,128]{3,2,1,0:T(8,128)S(1)}, u32[]{:S(2)}, u32[]{:S(2)}) %all-to-all-start) | async-done | bytes 524320 | tf_op jit(solution)/shard_map/all_to_all | solution.py:269
  22.9 0.0 copy-start.1
  22.9 7.2 %all-to-all-start.1 = ((f32[16,2,4,16,128]{4,3,2,1,0:T(8,128)}), f32[16,2,4,16,128]{4,3,2,1,0:T(8,128)S(1)}, u32[]{:S(2)}, u32[]{:S(2)}) async-start(f32[16,2,4,16,128]{4,3,2,1,0:T(8,128)} %pack_kinetic.1), calls=%async_computation.1 | async-start | bytes 2097152 | tf_op jit(solution)/shard_map/all_to_all | solution.py:270
  30.1 0.7 %slice_bitcast_fusion.1 = (f32[1,16,128]{2,1,0:T(8,128)S(1)}, f32[1,16,128]{2,1,0:T(8,128)S(1)}) fusion(f32[1,30,16,128]{3,2,1,0:T(8,128)} %param.6), kind=kLoop, calls=%fused_computation.10 | loop fusion | bytes 32768 | tf_op jit(solution)/shard_map/slice | solution.py:273
  30.8 1.6 %collective-permute-start.2 = (f32[1,2,16,128]{3,2,1,0:T(8,128)S(1)}, f32[1,2,16,128]{3,2,1,0:T(8,128)S(1)}, u32[]{:S(2)}, u32[]{:S(2)}) collective-permute-start(f32[1,2,16,128]{3,2,1,0:T(8,128)S(1)} %maximum_bitcast_fusion), channel_id=1, source_target_pairs={{0,16},{16,0},{32,48},{48,32},{64,80},{80,64},{96,112},{112,96},{1... | collective-permute-start | bytes 49160 | tf_op jit(solution)/shard_map/ppermute | solution.py:276
  32.4 0.0 copy-done.7
  32.4 1.9 %collective-permute-start = (f32[30,128]{1,0:T(8,128)S(1)}, f32[30,128]{1,0:T(8,128)S(1)}, u32[]{:S(2)}, u32[]{:S(2)}) collective-permute-start(f32[30,128]{1,0:T(8,128)S(1)} %copy-done.7), channel_id=1, source_target_pairs={{0,1},{1,2},{2,3},{3,4},{4,5},{5,6},{6,7},{7,8},{8,9},{9,10},{10,1... | collective-permute-start | bytes 46088 | tf_op jit(solution)/shard_map/ppermute | solution.py:271
  34.3 0.0 copy-done.6
  34.3 4.9 %collective-permute-start.1 = (f32[30,128]{1,0:T(8,128)S(1)}, f32[30,128]{1,0:T(8,128)S(1)}, u32[]{:S(2)}, u32[]{:S(2)}) collective-permute-start(f32[30,128]{1,0:T(8,128)S(1)} %copy-done.6), channel_id=1, source_target_pairs={{1,0},{2,1},{3,2},{4,3},{5,4},{6,5},{7,6},{8,7},{9,8},{10,9},{11,1... | collective-permute-start | bytes 46088 | tf_op jit(solution)/shard_map/ppermute | solution.py:272
  39.2 0.0 collective-permute-done.2
  39.2 3.0 %collective-permute-start.3 = (f32[2,2,16,128]{3,2,1,0:T(8,128)S(1)}, f32[2,2,16,128]{3,2,1,0:T(8,128)S(1)}, u32[]{:S(2)}, u32[]{:S(2)}) collective-permute-start(f32[2,2,16,128]{3,2,1,0:T(8,128)S(1)} %pad_maximum_fusion.2), channel_id=1, source_target_pairs={{0,32},{16,48},{32,0},{48,16},{64,96},{80,112},{96,64},{112,80},{1... | collective-permute-start | bytes 98312 | tf_op jit(solution)/shard_map/ppermute | solution.py:276
  42.2 0.0 copy-done.5
  42.2 0.7 %copy.7.contacts_ref = s32[16,2]{1,0:T(8,128)} copy(s32[16,2]{0,1:T(2,128)S(1)} %copy-done.5) | data formatting | bytes 256 | tf_op args[4]
  42.9 1.8 %collective-permute-done.3 = f32[2,2,16,128]{3,2,1,0:T(8,128)S(1)} collective-permute-done((f32[2,2,16,128]{3,2,1,0:T(8,128)S(1)}, f32[2,2,16,128]{3,2,1,0:T(8,128)S(1)}, u32[]{:S(2)}, u32[]{:S(2)}) %collective-permute-start.3) | collective-permute-done | bytes 32800 | tf_op jit(solution)/shard_map/ppermute | solution.py:276
  44.7 1.2 %collective-permute-start.4 = (f32[4,2,16,128]{3,2,1,0:T(8,128)S(1)}, f32[4,2,16,128]{3,2,1,0:T(8,128)S(1)}, u32[]{:S(2)}, u32[]{:S(2)}) collective-permute-start(f32[4,2,16,128]{3,2,1,0:T(8,128)S(1)} %pad_maximum_fusion.1), channel_id=1, source_target_pairs={{0,64},{16,80},{32,96},{48,112},{64,0},{80,16},{96,32},{112,48},{1... | collective-permute-start | bytes 196616 | tf_op jit(solution)/shard_map/ppermute | solution.py:276
  45.9 3.8 %collective-permute-done.4 = f32[4,2,16,128]{3,2,1,0:T(8,128)S(1)} collective-permute-done((f32[4,2,16,128]{3,2,1,0:T(8,128)S(1)}, f32[4,2,16,128]{3,2,1,0:T(8,128)S(1)}, u32[]{:S(2)}, u32[]{:S(2)}) %collective-permute-start.4) | collective-permute-done | bytes 65568 | tf_op jit(solution)/shard_map/ppermute | solution.py:276
  49.7 0.1 collective-permute-start.5
  49.8 6.4 %collective-permute-done.5 = f32[8,2,16,128]{3,2,1,0:T(8,128)S(1)} collective-permute-done((f32[8,2,16,128]{3,2,1,0:T(8,128)S(1)}, f32[8,2,16,128]{3,2,1,0:T(8,128)S(1)}, u32[]{:S(2)}, u32[]{:S(2)}) %collective-permute-start.5) | collective-permute-done | bytes 131104 | tf_op jit(solution)/shard_map/ppermute | solution.py:276
  56.3 0.0 copy-done.1
  56.3 0.0 copy-start.2
  56.3 7.5 %particle.1 = f32[4,10,256,128]{3,2,1,0:T(8,128)} custom-call(s32[16]{0:T(128)} %counts_ref.5, f32[4,10,256,128]{3,2,1,0:T(8,128)} %bitcast.16, f32[16,4,16,128]{3,2,1,0:T(8,128)} %copy-done.1, f32[4,256,128]{2,1,0:T(8,128)} %bitcast.20), custom_call_target="tpu_custom_call" | custom-call | flops 26214400 | bytes 10485760 | tf_op jit(solution)/shard_map/particle/pallas_call | solution.py:144
  63.7 0.0 copy-done.2
  63.7 0.0 collective-permute-done.low_ref
  63.8 0.0 copy-start.3
  63.8 0.0 collective-permute-done.1.high_ref
  63.8 0.0 copy-start.4
  63.8 0.0 all-to-all-done.1
  63.8 0.0 copy-start
  63.8 0.5 copy-done.3
  64.4 0.0 copy-done.4
  64.4 0.4 copy-done
  64.8 3.0 %column.1 = f32[30,16,128]{2,1,0:T(8,128)} custom-call(s32[16]{0:T(128)} %counts_ref.5, s32[16,2]{1,0:T(8,128)} %copy.7.contacts_ref, f32[30,16,128]{2,1,0:T(8,128)} %bitcast.22, f32[128,16,128]{2,1,0:T(8,128)} %bitcast.18, f32[30,128]{1,0:T(8,128)} %copy-done.3, f32[30,128]{1,0:T(8,128)} %copy-done.4, f32[16,2,16,128]{3,2,1,0:T(8,128)} %copy-done.2), custom_call_target="tpu_custom_call" | custom-call | flops 12288000 | bytes 491520 | tf_op jit(solution)/shard_map/column/pallas_call | solution.py:244
  (9 shorter events, 0.1 us)
Async XLA Ops:
  0.6 41.6 %copy-start.5 = (s32[16,2]{0,1:T(2,128)S(1)}, s32[16,2]{0,1:T(2,128)}, u32[]{:S(2)}) copy-start(s32[16,2]{0,1:T(2,128)} %param.9) | copy-start | bytes 388
  2.5 29.9 %copy-start.7 = (f32[30,128]{1,0:T(8,128)S(1)}, f32[30,128]{1,0:T(8,128)}, u32[]{:S(2)}) copy-start(f32[30,128]{1,0:T(8,128)} %get-tuple-element.6) | copy-start | bytes 46084
  2.5 31.8 %copy-start.6 = (f32[30,128]{1,0:T(8,128)S(1)}, f32[30,128]{1,0:T(8,128)}, u32[]{:S(2)}) copy-start(f32[30,128]{1,0:T(8,128)} %get-tuple-element.7) | copy-start | bytes 46084
  2.5 20.4 %all-to-all-start = ((f32[16,4,16,128]{3,2,1,0:T(8,128)}), f32[16,4,16,128]{3,2,1,0:T(8,128)S(1)}, u32[]{:S(2)}, u32[]{:S(2)}) async-start(f32[16,4,16,128]{3,2,1,0:T(8,128)} %bitcast.23), calls=%async_computation | async-start | bytes 1048576 | tf_op jit(solution)/shard_map/all_to_all | solution.py:269
  22.9 33.4 %copy-start.1 = (f32[16,4,16,128]{3,2,1,0:T(8,128)}, f32[16,4,16,128]{3,2,1,0:T(8,128)S(1)}, u32[]{:S(2)}) copy-start(f32[16,4,16,128]{3,2,1,0:T(8,128)S(1)} %all-to-all-done.rise_ref) | copy-start | bytes 1572868
  22.9 40.9 %all-to-all-start.1 = ((f32[16,2,4,16,128]{4,3,2,1,0:T(8,128)}), f32[16,2,4,16,128]{4,3,2,1,0:T(8,128)S(1)}, u32[]{:S(2)}, u32[]{:S(2)}) async-start(f32[16,2,4,16,128]{4,3,2,1,0:T(8,128)} %pack_kinetic.1), calls=%async_computation.1 | async-start | bytes 2097152 | tf_op jit(solution)/shard_map/all_to_all | solution.py:270
  30.8 8.4 %collective-permute-start.2 = (f32[1,2,16,128]{3,2,1,0:T(8,128)S(1)}, f32[1,2,16,128]{3,2,1,0:T(8,128)S(1)}, u32[]{:S(2)}, u32[]{:S(2)}) collective-permute-start(f32[1,2,16,128]{3,2,1,0:T(8,128)S(1)} %maximum_bitcast_fusion), channel_id=1, source_target_pairs={{0,16},{16,0},{32,48},{48,32},{64,80},{80,64},{96,112},{112,96},{1... | collective-permute-start | bytes 49160 | tf_op jit(solution)/shard_map/ppermute | solution.py:276
  32.4 31.4 %collective-permute-start = (f32[30,128]{1,0:T(8,128)S(1)}, f32[30,128]{1,0:T(8,128)S(1)}, u32[]{:S(2)}, u32[]{:S(2)}) collective-permute-start(f32[30,128]{1,0:T(8,128)S(1)} %copy-done.7), channel_id=1, source_target_pairs={{0,1},{1,2},{2,3},{3,4},{4,5},{5,6},{6,7},{7,8},{8,9},{9,10},{10,1... | collective-permute-start | bytes 46088 | tf_op jit(solution)/shard_map/ppermute | solution.py:271
  34.3 29.5 %collective-permute-start.1 = (f32[30,128]{1,0:T(8,128)S(1)}, f32[30,128]{1,0:T(8,128)S(1)}, u32[]{:S(2)}, u32[]{:S(2)}) collective-permute-start(f32[30,128]{1,0:T(8,128)S(1)} %copy-done.6), channel_id=1, source_target_pairs={{1,0},{2,1},{3,2},{4,3},{5,4},{6,5},{7,6},{8,7},{9,8},{10,9},{11,1... | collective-permute-start | bytes 46088 | tf_op jit(solution)/shard_map/ppermute | solution.py:272
  39.2 5.5 %collective-permute-start.3 = (f32[2,2,16,128]{3,2,1,0:T(8,128)S(1)}, f32[2,2,16,128]{3,2,1,0:T(8,128)S(1)}, u32[]{:S(2)}, u32[]{:S(2)}) collective-permute-start(f32[2,2,16,128]{3,2,1,0:T(8,128)S(1)} %pad_maximum_fusion.2), channel_id=1, source_target_pairs={{0,32},{16,48},{32,0},{48,16},{64,96},{80,112},{96,64},{112,80},{1... | collective-permute-start | bytes 98312 | tf_op jit(solution)/shard_map/ppermute | solution.py:276
  44.7 5.0 %collective-permute-start.4 = (f32[4,2,16,128]{3,2,1,0:T(8,128)S(1)}, f32[4,2,16,128]{3,2,1,0:T(8,128)S(1)}, u32[]{:S(2)}, u32[]{:S(2)}) collective-permute-start(f32[4,2,16,128]{3,2,1,0:T(8,128)S(1)} %pad_maximum_fusion.1), channel_id=1, source_target_pairs={{0,64},{16,80},{32,96},{48,112},{64,0},{80,16},{96,32},{112,48},{1... | collective-permute-start | bytes 196616 | tf_op jit(solution)/shard_map/ppermute | solution.py:276
  49.7 6.6 %collective-permute-start.5 = (f32[8,2,16,128]{3,2,1,0:T(8,128)S(1)}, f32[8,2,16,128]{3,2,1,0:T(8,128)S(1)}, u32[]{:S(2)}, u32[]{:S(2)}) collective-permute-start(f32[8,2,16,128]{3,2,1,0:T(8,128)S(1)} %pad_maximum_fusion), channel_id=1, source_target_pairs={{0,128},{16,144},{32,160},{48,176},{64,192},{80,208},{96,224},{112... | collective-permute-start | bytes 393224 | tf_op jit(solution)/shard_map/ppermute | solution.py:276
  56.3 7.5 %copy-start.2 = (f32[16,2,16,128]{3,2,1,0:T(8,128)}, f32[16,2,16,128]{3,2,1,0:T(8,128)S(1)}, u32[]{:S(2)}) copy-start(f32[16,2,16,128]{3,2,1,0:T(8,128)S(1)} %constant_dynamic-update-slice_fusion.faces_ref) | copy-start | bytes 786436
  63.8 0.6 copy-start.3
  63.8 0.6 copy-start.4
  63.8 1.0 %copy-start = (f32[16,2,4,16,128]{4,3,2,1,0:T(8,128)}, f32[16,2,4,16,128]{4,3,2,1,0:T(8,128)S(1)}, u32[]{:S(2)}) copy-start(f32[16,2,4,16,128]{4,3,2,1,0:T(8,128)S(1)} %all-to-all-done.1) | copy-start | bytes 3145732

commit v2 on v1

v2 whole, which is shorter than its diff:
```python
import functools

import jax
import jax.numpy as jnp
from jax import lax
from jax.experimental import pallas as pl
from jax.experimental.pallas import tpu as pltpu
from jax.sharding import PartitionSpec as P

BASE_KELVIN = 298.15
RATE_ACTIVATION = 5000.0
DIFFUSION_ACTIVATION = 3000.0
RATE_CONSTANT = 0.5
VOLT_PER_KELVIN = 2.0 * 8.314462618 / 96485.33212
HEAT_SCALE = 10.0
ENTROPY_SLOPE = 0.001
DIFFUSION_STEP = 0.005
SURFACE_STEP = 0.005
INPLANE_CONDUCT = 0.25
THROUGH_CONDUCT = 2.0
CONTACT_CONDUCT = 0.5

SMEM = pltpu.MemorySpace.SMEM
VMEM = pltpu.MemorySpace.VMEM
HBM = pltpu.MemorySpace.HBM


def reciprocal(value):
    return pl.reciprocal(value, approx=True)


def near(*arrays):
    return [pltpu.with_memory_space_constraint(array, VMEM) for array in arrays]


def far(*arrays):
    return [pltpu.with_memory_space_constraint(array, HBM) for array in arrays]


def params(mebibytes):
    return pltpu.CompilerParams(vmem_limit_bytes=mebibytes * 2**20)


def starts_of(counts_ref, devices):
    starts = [jnp.int32(0)]
    for d in range(devices):
        starts.append(starts[-1] + counts_ref[d])
    return starts


def pack_rise(heat_rise, layer_counts, contacts, slots):
    layers, rows, columns = heat_rise.shape
    devices = layer_counts.shape[0]
    cells = contacts.shape[1]

    def kernel(counts_ref, contacts_ref, heat_ref, send_ref, faces_ref):
        cell = lax.axis_index("cell")
        starts = starts_of(counts_ref, devices)
        for d in range(devices):
            for s in range(slots):
                layer = jnp.minimum(starts[d] + s, layers - 1)
                send_ref[d, s] = heat_ref[layer]
        for j in range(cells):
            faces_ref[j] = heat_ref[jnp.where(contacts_ref[0, j] == cell, layers - 1, 0)]

    return pl.pallas_call(
        kernel,
        name="pack_rise",
        out_shape=(
            VMEM((devices, slots, rows, columns), jnp.float32),
            VMEM((cells, rows, columns), jnp.float32),
        ),
        compiler_params=params(4),
        in_specs=[pl.BlockSpec(memory_space=SMEM)] * 2 + [pl.BlockSpec(memory_space=VMEM)],
        out_specs=[pl.BlockSpec(memory_space=VMEM)] * 2,
    )(layer_counts, contacts, *near(heat_rise))


def split_kinetic(shell_conc, layer_current, heat_rise, chips):
    slots, shells, rows, columns = shell_conc.shape
    layers, part, _ = heat_rise.shape
    blocks = chips * 2 * slots
    edges = -(-layers // part)

    def kernel(shell_ref, current_ref, heat_ref, mine_ref, theirs_ref, sem):
        core = lax.axis_index("sub") % 2
        copies = []
        for chip in range(chips):
            for turn, target in enumerate((theirs_ref, mine_ref)):
                side = 1 - core if turn == 0 else core
                here = pl.ds(pl.multiple_of((2 * chip + side) * part, part), part)
                for array, source in enumerate((shell_ref.at[:, shells - 1, here], current_ref.at[:, here])):
                    there = target.at[pl.ds((2 * chip + array) * slots, slots)]
                    copies.append(pltpu.make_async_copy(source, there, sem.at[len(copies)]))
        for copy in copies:
            copy.start()
        for layer in range(layers):
            block, row = layer // part, layer % part
            theirs_ref[blocks + block, row : row + 1] = heat_ref[layer, 0:1]
            theirs_ref[blocks + edges + block, row : row + 1] = heat_ref[layer, part - 1 : part]
        for copy in copies:
            copy.wait()

    return pl.pallas_call(
        kernel,
        name="split_kinetic",
        out_shape=(
            VMEM((blocks, part, columns), jnp.float32),
            VMEM((blocks + 2 * edges, part, columns), jnp.float32),
        ),
        compiler_params=params(4),
        in_specs=[pl.BlockSpec(memory_space=HBM)] * 2 + [pl.BlockSpec(memory_space=VMEM)],
        out_specs=[pl.BlockSpec(memory_space=VMEM)] * 2,
        scratch_shapes=[pltpu.SemaphoreType.DMA((4 * chips,))],
    )(*far(shell_conc, layer_current), *near(heat_rise))


def pack_kinetic(mine, got, hops):
    blocks, part, columns = mine.shape
    edges = (got.shape[0] - blocks) // 2
    chips = lax.axis_size("sub") // 2
    each = blocks // chips

    def kernel(mine_ref, got_ref, *send_refs):
        position = lax.axis_index("sub")
        chip, core = position // 2, position % 2
        for hop, send_ref in zip(hops, send_refs):
            target = lax.rem(chip + hop + chips, chips)
            send_ref[pl.ds(core * each, each)] = mine_ref[pl.ds(target * each, each)]
            send_ref[pl.ds((1 - core) * each, each)] = got_ref[pl.ds(target * each, each)]
            if abs(hop) == 1:
                first = blocks + (edges if hop == 1 else 0)
                send_ref[2 * each : 2 * each + edges] = got_ref[first : first + edges]

    return pl.pallas_call(
        kernel,
        name="pack_kinetic",
        out_shape=tuple(
            VMEM((2 * each + (edges if abs(hop) == 1 else 0), part, columns), jnp.float32)
            for hop in hops
        ),
        compiler_params=params(4),
        in_specs=[pl.BlockSpec(memory_space=VMEM)] * 2,
        out_specs=[pl.BlockSpec(memory_space=VMEM)] * len(hops),
    )(*near(mine, got))


def particle(shell_conc, slot_rise, layer_current, layer_counts, pieces=2, chunk=64):
    slots, shells, rows, columns = shell_conc.shape
    sources, _, part, _ = slot_rise.shape
    piece = rows // pieces
    volume = [((i + 1) ** 3 - i**3) / (3.0 * shells**3) for i in range(shells)]
    link = [DIFFUSION_STEP * ((i + 1) ** 2 / shells**2 * shells) for i in range(shells - 1)]

    def kernel(counts_ref, states_ref, rise_ref, current_ref, out_ref, shell_ref, made, sem, got_sem):
        fetches = [
            pltpu.make_async_copy(states_ref.at[slot], shell_ref.at[slot], got_sem.at[slot])
            for slot in range(slots)
        ]
        for fetch in fetches:
            fetch.start()
        count = counts_ref[lax.axis_index("sub")]

        def solve(slot, first):
            here = slice(first, first + chunk)
            rise = jnp.concatenate(
                [rise_ref[first // part + k, slot] for k in range(chunk // part)], axis=0
            )
            scaled = rise * (DIFFUSION_ACTIVATION / BASE_KELVIN)
            speedup = jnp.exp(scaled * reciprocal(BASE_KELVIN + rise))
            held = [None] * shells
            inverse = [None] * shells
            capacity = amount = upper = None
            for i in range(shells):
                gain = volume[i] * shell_ref[slot, i, here]
                if i == 0:
                    capacity, amount = volume[0], gain
                else:
                    capacity = volume[i] + upper * capacity
                    amount = gain + upper * amount
                if i < shells - 1:
                    flow = link[i] * speedup
                    inverse[i] = reciprocal(capacity + flow)
                    upper = flow * inverse[i]
                else:
                    amount = amount - SURFACE_STEP * current_ref[slot, here]
                    inverse[i] = reciprocal(capacity)
                held[i] = amount
            value = held[-1] * inverse[-1]
            made[slot, shells - 1, here] = value
            for i in range(shells - 2, -1, -1):
                value = inverse[i] * (held[i] + (link[i] * speedup) * value)
                made[slot, i, here] = value

        copies = []
        for slot in range(slots):
            fetches[slot].wait()
            for first in range(0, rows, piece):
                here = slice(first, first + piece)

                @pl.when(slot < count)
                def _(slot=slot, first=first):
                    for begin in range(first, first + piece, chunk):
                        solve(slot, begin)

                @pl.when(slot >= count)
                def _(slot=slot, here=here):
                    made[slot, :, here] = jnp.zeros((shells, piece, columns), jnp.float32)

                copies.append(
                    pltpu.make_async_copy(made.at[slot, :, here], out_ref.at[slot, :, here], sem.at[len(copies)])
                )
                copies[-1].start()
        for copy in copies:
            copy.wait()

    return pl.pallas_call(
        kernel,
        name="particle",
        out_shape=HBM(shell_conc.shape, jnp.float32),
        in_specs=[pl.BlockSpec(memory_space=SMEM), pl.BlockSpec(memory_space=HBM)]
        + [pl.BlockSpec(memory_space=VMEM)] * 2,
        out_specs=pl.BlockSpec(memory_space=HBM),
        scratch_shapes=[
            pltpu.VMEM(shell_conc.shape, jnp.float32),
            pltpu.VMEM(shell_conc.shape, jnp.float32),
            pltpu.SemaphoreType.DMA((slots * pieces,)),
            pltpu.SemaphoreType.DMA((slots,)),
        ],
        compiler_params=params(16),
        cost_estimate=pl.CostEstimate(
            flops=20 * slots * shells * rows * columns,
            bytes_accessed=8 * slots * shells * rows * columns,
            transcendentals=0,
        ),
    )(layer_counts, *far(shell_conc), *near(slot_rise, layer_current))


def inverse_sine(value):
    magnitude = jnp.abs(value)
    rooted = jnp.sqrt(1.0 + magnitude * magnitude)
    positive = jnp.log1p(magnitude + magnitude * magnitude / (1.0 + rooted))
    return jnp.where(value < 0.0, -positive, positive), rooted


def column(heat_rise, mine, got, arrived, hops, faces, after, layer_counts, contacts):
    layers, rows, columns = heat_rise.shape
    devices = layer_counts.shape[0]
    chips = devices // 2
    each = mine.shape[0] // chips
    slots = each // 2
    edges = -(-layers // rows)
    blocks = mine.shape[0]
    last = layers - 1

    def kernel(counts_ref, contacts_ref, _, heat_ref, mine_ref, got_ref, faces_ref, *refs):
        arrived_refs, (out_ref, place, kinetic_ref, slope_ref, right_ref) = refs[: len(hops)], refs[len(hops) :]
        position = lax.axis_index("sub")
        cell = lax.axis_index("cell")
        chip, core = position // 2, position % 2
        kinetic_ref[pl.ds(core * each, each)] = mine_ref[pl.ds(chip * each, each)]
        kinetic_ref[pl.ds((1 - core) * each, each)] = got_ref[pl.ds(chip * each, each)]
        for hop, ref in zip(hops, arrived_refs):
            kinetic_ref[hop % chips * 2 * each : (hop % chips + 1) * 2 * each] = ref[: 2 * each]
        starts = starts_of(counts_ref, devices)
        for d in range(devices):
            hop = lax.rem(chip - d // 2 + chips, chips)
            for s in range(slots):
                place[starts[d] + s] = (2 * hop + d % 2) * each + s
        from_low, from_high = arrived_refs[hops.index(1)], arrived_refs[hops.index(-1)]
        row_id = lax.broadcasted_iota(jnp.int32, (rows, columns), 0)
        lane_id = lax.broadcasted_iota(jnp.int32, (rows, columns), 1)
        for layer in range(layers):
            rise = heat_ref[layer]
            block, row = layer // rows, slice(layer % rows, layer % rows + 1)
            low_row = jnp.where(
                core == 0, from_low[2 * each + block, row], got_ref[blocks + edges + block, row]
            )
            high_row = jnp.where(core == 0, got_ref[blocks + block, row], from_high[2 * each + block, row])
            low_row = jnp.where(position == 0, rise[0:1], low_row)
            high_row = jnp.where(position == devices - 1, rise[rows - 1 : rows], high_row)
            laplace = (
                jnp.where(row_id == 0, low_row, pltpu.roll(rise, 1, 0))
                + jnp.where(row_id == rows - 1, high_row, pltpu.roll(rise, rows - 1, 0))
                + jnp.where(lane_id == 0, rise, pltpu.roll(rise, 1, 1))
                + jnp.where(lane_id == columns - 1, rise, pltpu.roll(rise, columns - 1, 1))
                - 4.0 * rise
            )
            where = place[layer]
            surface = kinetic_ref[where]
            current = kinetic_ref[where + slots]
            kelvin = BASE_KELVIN + rise
            inverse_kelvin = 1.0 / kelvin
            base_rate = (
                RATE_CONSTANT
                * jnp.exp((RATE_ACTIVATION / BASE_KELVIN) * rise * inverse_kelvin)
                * jnp.sqrt(surface * (1.0 - surface))
            )
            ratio_rate = current / (2.0 * base_rate)
            arcsine, rooted = inverse_sine(ratio_rate)
            entropic = ENTROPY_SLOPE * (0.5 - surface)
            drive = VOLT_PER_KELVIN * arcsine + entropic
            scaled = HEAT_SCALE * current
            source = scaled * (kelvin * drive)
            slope = scaled * (
                drive - (VOLT_PER_KELVIN * RATE_ACTIVATION) * ratio_rate * inverse_kelvin / rooted
            )
            right = rise + INPLANE_CONDUCT * laplace + source - slope * rise
            if layer == 0 or layer == last:
                side = 0 if layer == 0 else 1
                partner = contacts_ref[side, cell]
                face = faces_ref[jnp.maximum(partner, 0)]
                face = jnp.where(partner >= 0, face, 0.0)
                right = right + CONTACT_CONDUCT * (face - rise)
            slope_ref[layer] = slope
            right_ref[layer] = right
        upper = value = None
        for layer in range(layers):
            diagonal = 1.0 - slope_ref[layer]
            source = right_ref[layer]
            if layer > 0:
                diagonal = diagonal + THROUGH_CONDUCT - THROUGH_CONDUCT * upper
                source = source + THROUGH_CONDUCT * value
            if layer < last:
                diagonal = diagonal + THROUGH_CONDUCT
            inverse = 1.0 / diagonal
            upper = THROUGH_CONDUCT * inverse
            value = source * inverse
            slope_ref[layer] = upper
            right_ref[layer] = value
        out_ref[last] = value
        for layer in range(last - 1, -1, -1):
            value = right_ref[layer] + slope_ref[layer] * value
            out_ref[layer] = value

    return pl.pallas_call(
        kernel,
        name="column",
        out_shape=jax.ShapeDtypeStruct(heat_rise.shape, jnp.float32),
        in_specs=[pl.BlockSpec(memory_space=SMEM)] * 2
        + [pl.BlockSpec(memory_space=HBM)]
        + [pl.BlockSpec(memory_space=VMEM)] * (4 + len(hops)),
        out_specs=pl.BlockSpec(memory_space=VMEM),
        scratch_shapes=[
            pltpu.SMEM((layers + slots,), jnp.int32),
            pltpu.VMEM((2 * blocks, rows, columns), jnp.float32),
            pltpu.VMEM((layers, rows, columns), jnp.float32),
            pltpu.VMEM((layers, rows, columns), jnp.float32),
        ],
        compiler_params=params(8),
        cost_estimate=pl.CostEstimate(
            flops=200 * layers * rows * columns, bytes_accessed=8 * layers * rows * columns, transcendentals=0
        ),
    )(layer_counts, contacts, *far(after), *near(heat_rise, mine, got, faces, *arrived))


def per_device(shell_conc, heat_rise, layer_current, layer_counts, contacts):
    shell_conc, heat_rise, layer_current = shell_conc[0], heat_rise[0], layer_current[0]
    slots = shell_conc.shape[0]
    layers, part, columns = heat_rise.shape
    devices = lax.axis_size("sub")
    chips = devices // 2
    hops = (1, -1, 2, -2, 3, -3, 4)
    contacts = contacts.T
    mine, theirs = split_kinetic(shell_conc, layer_current, heat_rise, chips)
    theirs, heat_behind = lax.optimization_barrier((theirs, heat_rise))
    send_rise, send_faces = pack_rise(heat_behind, layer_counts, contacts, slots)
    got_rise = lax.all_to_all(send_rise, "sub", 0, 0)
    got = lax.ppermute(theirs, "sub", [(i, i ^ 1) for i in range(devices)])
    arrived = [
        lax.ppermute(message, "sub", [(i, (i + 2 * hop) % devices) for i in range(devices)])
        for hop, message in zip(hops, pack_kinetic(mine, got, hops))
    ]
    got_rise, send_faces = lax.optimization_barrier((got_rise, send_faces))
    faces = lax.all_to_all(send_faces, "cell", 0, 0, tiled=True)
    conc_new = particle(shell_conc, got_rise, layer_current, layer_counts)
    heat_new = column(heat_rise, mine, got, arrived, hops, faces, conc_new, layer_counts, contacts)
    return conc_new[None], heat_new[None]


def solution(mesh):
    in_specs = (
        P("cell", "sub", None, None, None),
        P("cell", None, "sub", None),
        P("cell", "sub", None, None),
        P(),
        P(),
    )
    out_specs = (P("cell", "sub", None, None, None), P("cell", None, "sub", None))
    return jax.shard_map(
        per_device, mesh=mesh, in_specs=in_specs, out_specs=out_specs, check_vma=False
    )
```

time: 68.8 us -> 57.8 us (0.84)
  the two profiles are of different devices: /device:TPU:132 before, /device:TPU:2 now
where the time goes in v2:
time: 57.8 us; the launch traced here: 57.5 us
  starting transfers between devices  32.5 us (56%)
  waiting for transfers between devices  11.5 us (20%)
  Pallas kernels  11.1 us (19%)
  local copies, waits for them, and re-layouts  1.61 us (3%)
  between operations  0.76 us (1%)
    ppermute x7, starting transfers between devices, per_device(): lax.ppermute(message, 'sub', [(i, (i + 2 * hop) % devices) for i in range...  16 us
    ppermute x7, waiting for transfers between devices, per_device(): lax.ppermute(message, 'sub', [(i, (i + 2 * hop) % devices) for i in range...  8.6 us
    all_to_all x1, starting transfers between devices, per_device(): got_rise = lax.all_to_all(send_rise, 'sub', 0, 0)  8.57 us
    all_to_all x1, starting transfers between devices, per_device(): faces = lax.all_to_all(send_faces, 'cell', 0, 0, tiled=True)  7.48 us
    pallas_call x1, Pallas kernels, particle(): pl.pallas_call(kernel, name='particle', out_shape=HBM(shell_conc.shape, j...  5.07 us
    pallas_call x1, Pallas kernels, column(): pl.pallas_call(kernel, name='column', out_shape=jax.ShapeDtypeStruct(heat...  2.18 us
    ppermute x1, waiting for transfers between devices, per_device(): got = lax.ppermute(theirs, 'sub', [(i, i ^ 1) for i in range(devices)])  1.63 us
    unnamed x12, local copies, waits for them, and re-layouts  1.61 us
  transfers between devices with their start and end apart: 10, of which 3 were waited for; matrix products, arithmetic and copies ran while one was open for 0% of the time, Pallas kernels for 10%

profile of v2, /device:TPU:2, one launch (start us, length us, event | category | flops | bytes accessed | tf_op | source)
XLA Modules:
  0.0 57.5 jit_solution(11244205912202098023)
XLA Ops:
  0.6 0.0 copy-start.5
  0.6 0.0 copy-start.4
  0.7 0.0 copy-start
  0.7 0.9 %copy-done = f32[1,30,16,128]{3,2,1,0:T(8,128)S(1)} copy-done((f32[1,30,16,128]{3,2,1,0:T(8,128)S(1)}, f32[1,30,16,128]{3,2,1,0:T(8,128)}, u32[]{:S(2)}) %copy-start) | copy-done | bytes 245784
  1.6 0.0 copy-start.1
  1.6 0.0 copy-start.2
  1.6 1.5 %split_kinetic.1 = (f32[64,16,128]{2,1,0:T(8,128)S(1)}, f32[68,16,128]{2,1,0:T(8,128)S(1)}) custom-call(f32[4,10,256,128]{3,2,1,0:T(8,128)} %bitcast.13, f32[4,256,128]{2,1,0:T(8,128)} %bitcast.9, f32[30,16,128]{2,1,0:T(8,128)S(1)} %bitcast.6), custom_call_target="tpu_custom_call" | custom-call | tf_op jit(solution)/shard_map/split_kinetic/pallas_call | solution.py:104
  3.1 0.0 copy-done.5
  3.2 0.0 copy-done.4
  3.2 0.0 copy-done.1
  3.2 1.5 %pack_rise.1 = (f32[16,4,16,128]{3,2,1,0:T(8,128)}, f32[16,16,128]{2,1,0:T(8,128)S(1)}) custom-call(s32[16]{0:T(128)S(1)} %copy-done.4, s32[2,16]{1,0:T(2,128)S(1)} %bitcast.11, f32[30,16,128]{2,1,0:T(8,128)S(1)} %bitcast.7), custom_call_target="tpu_custom_call" | custom-call | tf_op jit(solution)/shard_map/pack_rise/pallas_call | solution.py:66
  4.6 0.0 copy-start.3
  4.6 0.6 %copy-done.3 = f32[16,16,128]{2,1,0:T(8,128)} copy-done((f32[16,16,128]{2,1,0:T(8,128)}, f32[16,16,128]{2,1,0:T(8,128)S(1)}, u32[]{:S(2)}) %copy-start.3) | copy-done | bytes 131096
  5.3 8.6 %all-to-all-start = ((f32[16,4,16,128]{3,2,1,0:T(8,128)}), f32[16,4,16,128]{3,2,1,0:T(8,128)S(1)}, u32[]{:S(2)}, u32[]{:S(2)}) async-start(f32[16,4,16,128]{3,2,1,0:T(8,128)} %get-tuple-element.19), calls=%async_computation | async-start | bytes 1048576 | tf_op jit(solution)/shard_map/all_to_all | solution.py:368
  13.9 0.4 collective-permute-start
  14.3 1.6 %collective-permute-done.got_ref = f32[68,16,128]{2,1,0:T(8,128)S(1)} collective-permute-done((f32[68,16,128]{2,1,0:T(8,128)S(1)}, f32[68,16,128]{2,1,0:T(8,128)S(1)}, u32[]{:S(2)}, u32[]{:S(2)}) %collective-permute-start) | collective-permute-done | bytes 557088 | tf_op jit(solution)/shard_map/ppermute | solution.py:369
  15.9 0.9 %pack_kinetic.1 = (f32[18,16,128]{2,1,0:T(8,128)}, f32[18,16,128]{2,1,0:T(8,128)}, f32[16,16,128]{2,1,0:T(8,128)S(1)}, f32[16,16,128]{2,1,0:T(8,128)S(1)}, f32[1...) custom-call(f32[64,16,128]{2,1,0:T(8,128)S(1)} %get-tuple-element.22.mine_ref, ...), custom_call_target="tpu_custom_call" | custom-call | tf_op jit(solution)/shard_map/pack_kinetic/pallas_call | solution.py:135
  16.8 2.7 %collective-permute-start.3 = (f32[16,16,128]{2,1,0:T(8,128)S(1)}, f32[16,16,128]{2,1,0:T(8,128)S(1)}, u32[]{:S(2)}, u32[]{:S(2)}) collective-permute-start(f32[16,16,128]{2,1,0:T(8,128)S(1)} %get-tuple-element.27), channel_id=1, source_target_pairs={{0,4},{1,5},{2,6},{3,7},{4,8},{5,9},{6,10},{7,11},{8,12},{9,13},{1... | collective-permute-start | bytes 393224 | tf_op jit(solution)/shard_map/ppermute | solution.py:371
  19.5 1.4 %collective-permute-start.4 = (f32[16,16,128]{2,1,0:T(8,128)S(1)}, f32[16,16,128]{2,1,0:T(8,128)S(1)}, u32[]{:S(2)}, u32[]{:S(2)}) collective-permute-start(f32[16,16,128]{2,1,0:T(8,128)S(1)} %get-tuple-element.28), channel_id=1, source_target_pairs={{0,12},{1,13},{2,14},{3,15},{4,0},{5,1},{6,2},{7,3},{8,4},{9,5},{1... | collective-permute-start | bytes 393224 | tf_op jit(solution)/shard_map/ppermute | solution.py:371
  20.9 1.8 %collective-permute-start.1 = (f32[18,16,128]{2,1,0:T(8,128)}, f32[18,16,128]{2,1,0:T(8,128)S(1)}, u32[]{:S(2)}, u32[]{:S(2)}) collective-permute-start(f32[18,16,128]{2,1,0:T(8,128)} %get-tuple-element.25), channel_id=1, source_target_pairs={{0,2},{1,3},{2,4},{3,5},{4,6},{5,7},{6,8},{7,9},{8,10},{9,11},{10,... | collective-permute-start | bytes 442376 | tf_op jit(solution)/shard_map/ppermute | solution.py:371
  22.8 1.4 %collective-permute-start.2 = (f32[18,16,128]{2,1,0:T(8,128)}, f32[18,16,128]{2,1,0:T(8,128)S(1)}, u32[]{:S(2)}, u32[]{:S(2)}) collective-permute-start(f32[18,16,128]{2,1,0:T(8,128)} %get-tuple-element.26), channel_id=1, source_target_pairs={{0,14},{1,15},{2,0},{3,1},{4,2},{5,3},{6,4},{7,5},{8,6},{9,7},{10,... | collective-permute-start | bytes 442376 | tf_op jit(solution)/shard_map/ppermute | solution.py:371
  24.2 3.1 %collective-permute-start.5 = (f32[16,16,128]{2,1,0:T(8,128)}, f32[16,16,128]{2,1,0:T(8,128)S(1)}, u32[]{:S(2)}, u32[]{:S(2)}) collective-permute-start(f32[16,16,128]{2,1,0:T(8,128)} %get-tuple-element.29), channel_id=1, source_target_pairs={{0,6},{1,7},{2,8},{3,9},{4,10},{5,11},{6,12},{7,13},{8,14},{9,15},... | collective-permute-start | bytes 393224 | tf_op jit(solution)/shard_map/ppermute | solution.py:371
  27.3 8.6 %collective-permute-done.3.refs_2_ = f32[16,16,128]{2,1,0:T(8,128)S(1)} collective-permute-done((f32[16,16,128]{2,1,0:T(8,128)S(1)}, f32[16,16,128]{2,1,0:T(8,128)S(1)}, u32[]{:S(2)}, u32[]{:S(2)}) %collective-permute-start.3) | collective-permute-done | bytes 131104 | tf_op jit(solution)/shard_map/ppermute | solution.py:371
  35.8 2.3 %collective-permute-start.6 = (f32[16,16,128]{2,1,0:T(8,128)}, f32[16,16,128]{2,1,0:T(8,128)S(1)}, u32[]{:S(2)}, u32[]{:S(2)}) collective-permute-start(f32[16,16,128]{2,1,0:T(8,128)} %get-tuple-element.30), channel_id=1, source_target_pairs={{0,10},{1,11},{2,12},{3,13},{4,14},{5,15},{6,0},{7,1},{8,2},{9,3},... | collective-permute-start | bytes 393224 | tf_op jit(solution)/shard_map/ppermute | solution.py:371
  38.2 0.0 collective-permute-done.4.refs_3_
  38.2 3.2 %collective-permute-start.7 = (f32[16,16,128]{2,1,0:T(8,128)}, f32[16,16,128]{2,1,0:T(8,128)S(1)}, u32[]{:S(2)}, u32[]{:S(2)}) collective-permute-start(f32[16,16,128]{2,1,0:T(8,128)} %get-tuple-element.31), channel_id=1, source_target_pairs={{0,8},{1,9},{2,10},{3,11},{4,12},{5,13},{6,14},{7,15},{8,0},{9,1},... | collective-permute-start | bytes 393224 | tf_op jit(solution)/shard_map/ppermute | solution.py:371
  41.4 0.0 all-to-all-done.rise_ref
  41.4 7.5 %all-to-all-start.1 = ((f32[16,16,128]{2,1,0:T(8,128)}), f32[16,16,128]{2,1,0:T(8,128)S(1)}, u32[]{:S(2)}, u32[]{:S(2)}) async-start(f32[16,16,128]{2,1,0:T(8,128)} %copy-done.3), calls=%async_computation.1 | async-start | bytes 262144 | tf_op jit(solution)/shard_map/all_to_all | solution.py:375
  48.9 0.0 copy-done.2
  48.9 5.1 %particle.1._ = f32[4,10,256,128]{3,2,1,0:T(8,128)} custom-call(s32[16]{0:T(128)S(1)} %copy-done.4, f32[4,10,256,128]{3,2,1,0:T(8,128)} %bitcast.14, f32[16,4,16,128]{3,2,1,0:T(8,128)S(1)} %all-to-all-done.rise_ref, f32[4,256,128]{2,1,0:T(8,128)S(1)} %bitcast.10), custom_call_target="tpu_custom_call" | custom-call | flops 26214400 | bytes 10485760 | tf_op jit(solution)/shard_map/particle/pallas_call | solution.py:217
  54.0 0.0 collective-permute-done.5.refs_4_
  54.0 0.0 collective-permute-done.6.refs_5_
  54.0 0.0 collective-permute-done.7.refs_6_
  54.0 0.0 collective-permute-done.1.refs_0_
  54.0 0.0 collective-permute-done.2.refs_1_
  54.0 1.3 %all-to-all-done.1.faces_ref = f32[16,16,128]{2,1,0:T(8,128)S(1)} async-done(((f32[16,16,128]{2,1,0:T(8,128)}), f32[16,16,128]{2,1,0:T(8,128)S(1)}, u32[]{:S(2)}, u32[]{:S(2)}) %all-to-all-start.1) | async-done | bytes 131104 | tf_op jit(solution)/shard_map/all_to_all | solution.py:375
  55.3 2.2 %column.1 = f32[30,16,128]{2,1,0:T(8,128)} custom-call(s32[16]{0:T(128)S(1)} %copy-done.4, s32[2,16]{1,0:T(2,128)S(1)} %bitcast.12, f32[4,10,256,128]{3,2,1,0:T(8,128)} %particle.1._, f32[30,16,128]{2,1,0:T(8,128)S(1)} %bitcast.8, f32[64,16,128]{2,1,0:T(8,128)S(1)} %get-tuple-element.22.mine_ref, f32[68,16,128]{2,1,0:T(8,128)S(1)} %collective-permute-done.got_ref, ...), custom_call_target="tpu_custom_call" | custom-call | flops 12288000 | bytes 491520 | tf_op jit(solution)/shard_map/column/pallas_call | solution.py:336
Async XLA Ops:
  0.6 2.5 %copy-start.5 = (s32[16,2]{0,1:T(2,128)S(1)}, s32[16,2]{0,1:T(2,128)}, u32[]{:S(2)}) copy-start(s32[16,2]{0,1:T(2,128)} %param.9) | copy-start | bytes 388
  0.6 2.5 %copy-start.4 = (s32[16]{0:T(128)S(1)}, s32[16]{0:T(128)}, u32[]{:S(2)}) copy-start(s32[16]{0:T(128)} %counts_ref.5) | copy-start | bytes 196
  0.7 1.0 %copy-start = (f32[1,30,16,128]{3,2,1,0:T(8,128)S(1)}, f32[1,30,16,128]{3,2,1,0:T(8,128)}, u32[]{:S(2)}) copy-start(f32[1,30,16,128]{3,2,1,0:T(8,128)} %param.6) | copy-start | bytes 737284
  1.6 1.6 %copy-start.1 = (f32[1,30,16,128]{3,2,1,0:T(8,128)S(1)}, f32[1,30,16,128]{3,2,1,0:T(8,128)}, u32[]{:S(2)}) copy-start(f32[1,30,16,128]{3,2,1,0:T(8,128)} %param.6) | copy-start | bytes 737284
  1.6 47.3 %copy-start.2 = (f32[1,4,256,128]{3,2,1,0:T(8,128)S(1)}, f32[1,4,256,128]{3,2,1,0:T(8,128)}, u32[]{:S(2)}) copy-start(f32[1,4,256,128]{3,2,1,0:T(8,128)} %param.7) | copy-start | bytes 1572868
  4.6 0.6 %copy-start.3 = (f32[16,16,128]{2,1,0:T(8,128)}, f32[16,16,128]{2,1,0:T(8,128)S(1)}, u32[]{:S(2)}) copy-start(f32[16,16,128]{2,1,0:T(8,128)S(1)} %get-tuple-element.24) | copy-start | bytes 393220
  5.3 36.1 %all-to-all-start = ((f32[16,4,16,128]{3,2,1,0:T(8,128)}), f32[16,4,16,128]{3,2,1,0:T(8,128)S(1)}, u32[]{:S(2)}, u32[]{:S(2)}) async-start(f32[16,4,16,128]{3,2,1,0:T(8,128)} %get-tuple-element.19), calls=%async_computation | async-start | bytes 1048576 | tf_op jit(solution)/shard_map/all_to_all | solution.py:368
  13.9 2.0 %collective-permute-start = (f32[68,16,128]{2,1,0:T(8,128)S(1)}, f32[68,16,128]{2,1,0:T(8,128)S(1)}, u32[]{:S(2)}, u32[]{:S(2)}) collective-permute-start(f32[68,16,128]{2,1,0:T(8,128)S(1)} %get-tuple-element.23), channel_id=1, source_target_pairs={{0,1},{1,0},{2,3},{3,2},{4,5},{5,4},{6,7},{7,6},{8,9},{9,8},{10,11... | collective-permute-start | bytes 1671176 | tf_op jit(solution)/shard_map/ppermute | solution.py:369
  16.8 19.0 %collective-permute-start.3 = (f32[16,16,128]{2,1,0:T(8,128)S(1)}, f32[16,16,128]{2,1,0:T(8,128)S(1)}, u32[]{:S(2)}, u32[]{:S(2)}) collective-permute-start(f32[16,16,128]{2,1,0:T(8,128)S(1)} %get-tuple-element.27), channel_id=1, source_target_pairs={{0,4},{1,5},{2,6},{3,7},{4,8},{5,9},{6,10},{7,11},{8,12},{9,13},{1... | collective-permute-start | bytes 393224 | tf_op jit(solution)/shard_map/ppermute | solution.py:371
  19.5 18.6 %collective-permute-start.4 = (f32[16,16,128]{2,1,0:T(8,128)S(1)}, f32[16,16,128]{2,1,0:T(8,128)S(1)}, u32[]{:S(2)}, u32[]{:S(2)}) collective-permute-start(f32[16,16,128]{2,1,0:T(8,128)S(1)} %get-tuple-element.28), channel_id=1, source_target_pairs={{0,12},{1,13},{2,14},{3,15},{4,0},{5,1},{6,2},{7,3},{8,4},{9,5},{1... | collective-permute-start | bytes 393224 | tf_op jit(solution)/shard_map/ppermute | solution.py:371
  20.9 33.1 %collective-permute-start.1 = (f32[18,16,128]{2,1,0:T(8,128)}, f32[18,16,128]{2,1,0:T(8,128)S(1)}, u32[]{:S(2)}, u32[]{:S(2)}) collective-permute-start(f32[18,16,128]{2,1,0:T(8,128)} %get-tuple-element.25), channel_id=1, source_target_pairs={{0,2},{1,3},{2,4},{3,5},{4,6},{5,7},{6,8},{7,9},{8,10},{9,11},{10,... | collective-permute-start | bytes 442376 | tf_op jit(solution)/shard_map/ppermute | solution.py:371
  22.8 31.2 %collective-permute-start.2 = (f32[18,16,128]{2,1,0:T(8,128)}, f32[18,16,128]{2,1,0:T(8,128)S(1)}, u32[]{:S(2)}, u32[]{:S(2)}) collective-permute-start(f32[18,16,128]{2,1,0:T(8,128)} %get-tuple-element.26), channel_id=1, source_target_pairs={{0,14},{1,15},{2,0},{3,1},{4,2},{5,3},{6,4},{7,5},{8,6},{9,7},{10,... | collective-permute-start | bytes 442376 | tf_op jit(solution)/shard_map/ppermute | solution.py:371
  24.2 29.8 %collective-permute-start.5 = (f32[16,16,128]{2,1,0:T(8,128)}, f32[16,16,128]{2,1,0:T(8,128)S(1)}, u32[]{:S(2)}, u32[]{:S(2)}) collective-permute-start(f32[16,16,128]{2,1,0:T(8,128)} %get-tuple-element.29), channel_id=1, source_target_pairs={{0,6},{1,7},{2,8},{3,9},{4,10},{5,11},{6,12},{7,13},{8,14},{9,15},... | collective-permute-start | bytes 393224 | tf_op jit(solution)/shard_map/ppermute | solution.py:371
  35.8 18.1 %collective-permute-start.6 = (f32[16,16,128]{2,1,0:T(8,128)}, f32[16,16,128]{2,1,0:T(8,128)S(1)}, u32[]{:S(2)}, u32[]{:S(2)}) collective-permute-start(f32[16,16,128]{2,1,0:T(8,128)} %get-tuple-element.30), channel_id=1, source_target_pairs={{0,10},{1,11},{2,12},{3,13},{4,14},{5,15},{6,0},{7,1},{8,2},{9,3},... | collective-permute-start | bytes 393224 | tf_op jit(solution)/shard_map/ppermute | solution.py:371
  38.2 15.8 %collective-permute-start.7 = (f32[16,16,128]{2,1,0:T(8,128)}, f32[16,16,128]{2,1,0:T(8,128)S(1)}, u32[]{:S(2)}, u32[]{:S(2)}) collective-permute-start(f32[16,16,128]{2,1,0:T(8,128)} %get-tuple-element.31), channel_id=1, source_target_pairs={{0,8},{1,9},{2,10},{3,11},{4,12},{5,13},{6,14},{7,15},{8,0},{9,1},... | collective-permute-start | bytes 393224 | tf_op jit(solution)/shard_map/ppermute | solution.py:371
  41.4 13.9 %all-to-all-start.1 = ((f32[16,16,128]{2,1,0:T(8,128)}), f32[16,16,128]{2,1,0:T(8,128)S(1)}, u32[]{:S(2)}, u32[]{:S(2)}) async-start(f32[16,16,128]{2,1,0:T(8,128)} %copy-done.3), calls=%async_computation.1 | async-start | bytes 262144 | tf_op jit(solution)/shard_map/all_to_all | solution.py:375

commit v3 on v2

v3 whole, which is shorter than its diff:
```python
import functools

import jax
import jax.numpy as jnp
from jax import lax
from jax.experimental import pallas as pl
from jax.experimental.pallas import tpu as pltpu
from jax.sharding import PartitionSpec as P

BASE_KELVIN = 298.15
RATE_ACTIVATION = 5000.0
DIFFUSION_ACTIVATION = 3000.0
RATE_CONSTANT = 0.5
VOLT_PER_KELVIN = 2.0 * 8.314462618 / 96485.33212
HEAT_SCALE = 10.0
ENTROPY_SLOPE = 0.001
DIFFUSION_STEP = 0.005
SURFACE_STEP = 0.005
INPLANE_CONDUCT = 0.25
THROUGH_CONDUCT = 2.0
CONTACT_CONDUCT = 0.5

SMEM = pltpu.MemorySpace.SMEM
VMEM = pltpu.MemorySpace.VMEM
HBM = pltpu.MemorySpace.HBM


def reciprocal(value):
    return pl.reciprocal(value, approx=True)


def near(*arrays):
    return [pltpu.with_memory_space_constraint(array, VMEM) for array in arrays]


def far(*arrays):
    return [pltpu.with_memory_space_constraint(array, HBM) for array in arrays]


def params(mebibytes):
    return pltpu.CompilerParams(vmem_limit_bytes=mebibytes * 2**20)


def starts_of(counts_ref, devices):
    starts = [jnp.int32(0)]
    for d in range(devices):
        starts.append(starts[-1] + counts_ref[d])
    return starts


def along(hop, chips):
    return [
        pair
        for z in range(chips)
        for pair in ((2 * z, 2 * ((z + hop) % chips)), (2 * z + 1, 2 * ((z - hop) % chips) + 1))
    ]


def place_of():
    position = lax.axis_index("sub")
    core = position % 2
    return position, position // 2, core, 1 - 2 * core


def pair_counts(counts_ref, chip):
    return counts_ref[2 * chip], counts_ref[2 * chip + 1]


def split_kinetic(shell_conc, layer_current, chips):
    slots, shells, rows, columns = shell_conc.shape
    pair = rows // chips
    part = pair // 2
    hops = chips // 2

    def kernel(shell_ref, current_ref, mine_ref, theirs_ref, sem):
        position, chip, core, sign = place_of()
        copies = []
        for turn, target in enumerate((theirs_ref, mine_ref)):
            way = -sign if turn == 0 else sign
            side = 1 - core if turn == 0 else core
            for array, source in enumerate((shell_ref.at[:, shells - 1], current_ref)):
                for hop in range(1, hops):
                    to = lax.rem(chip + way * hop + chips, chips)
                    here = pl.ds(pl.multiple_of(to * pair, pair), pair)
                    there = target.at[pl.ds(((hop - 1) * 2 + array) * slots, slots)]
                    copies.append((source.at[:, here], there))
                for half, to in enumerate((chip, lax.rem(chip + hops, chips))):
                    here = pl.ds(pl.multiple_of(to * pair + side * part, part), part)
                    there = target.at[
                        pl.ds(((hops - 1) * 2 + array) * slots, slots), pl.ds(half * part, part)
                    ]
                    copies.append((source.at[:, here], there))
        copies = [pltpu.make_async_copy(*copy, sem.at[i]) for i, copy in enumerate(copies)]
        for copy in copies:
            copy.start()
        for copy in copies:
            copy.wait()

    return pl.pallas_call(
        kernel,
        name="split_kinetic",
        out_shape=(VMEM((hops * 2 * slots, pair, columns), jnp.float32),) * 2,
        compiler_params=params(4),
        in_specs=[pl.BlockSpec(memory_space=HBM)] * 2,
        out_specs=[pl.BlockSpec(memory_space=VMEM)] * 2,
        scratch_shapes=[pltpu.SemaphoreType.DMA((4 * (hops + 1),))],
    )(*far(shell_conc, layer_current))


def pack_rise(heat_rise, other_rise, layer_counts, contacts, room):
    layers, part, columns = heat_rise.shape
    devices = layer_counts.shape[0]
    chips, cells = devices // 2, contacts.shape[1]
    hops = chips // 2

    def kernel(counts_ref, contacts_ref, heat_ref, other_ref, *refs):
        send_refs, (faces_ref, table) = refs[:hops], refs[hops:]
        position, chip, core, sign = place_of()
        cell = lax.axis_index("cell")
        starts = starts_of(counts_ref, devices)
        for to in range(chips):
            table[to] = starts[2 * to]
        ours = pl.ds(pl.multiple_of(core * part, part), part)
        others = pl.ds(pl.multiple_of((1 - core) * part, part), part)
        for hop, send_ref in zip(range(1, hops + 1), send_refs):
            start = table[lax.rem(chip + sign * hop + chips, chips)]
            for j in range(room):
                layer = jnp.minimum(start + j, layers - 1)
                if hop < hops:
                    send_ref[j, ours] = heat_ref[layer]
                    send_ref[j, others] = other_ref[layer]
                else:
                    send_ref[j] = heat_ref[layer]
        for layer in range(layers):
            send_refs[0][room, layer : layer + 1] = jnp.where(
                core == 0, other_ref[layer, part - 1 : part], other_ref[layer, 0:1]
            )
        for j in range(cells):
            faces_ref[j] = heat_ref[jnp.where(contacts_ref[0, j] == cell, layers - 1, 0)]

    return pl.pallas_call(
        kernel,
        name="pack_rise",
        out_shape=(
            VMEM((room + 1, 2 * part, columns), jnp.float32),
            *[VMEM((room, 2 * part, columns), jnp.float32)] * (hops - 2),
            VMEM((room, part, columns), jnp.float32),
            VMEM((cells, part, columns), jnp.float32),
        ),
        compiler_params=params(4),
        in_specs=[pl.BlockSpec(memory_space=SMEM)] * 2 + [pl.BlockSpec(memory_space=VMEM)] * 2,
        out_specs=[pl.BlockSpec(memory_space=VMEM)] * (hops + 1),
        scratch_shapes=[pltpu.SMEM((chips,), jnp.int32)],
    )(layer_counts, contacts, *near(heat_rise, other_rise))


def pack_kinetic(mine, got, layer_counts, room):
    blocks, pair, columns = mine.shape
    hops = layer_counts.shape[0] // 4
    slots = blocks // (2 * hops)
    part = pair // 2

    def kernel(counts_ref, mine_ref, got_ref, *refs):
        send_refs, (home_ref, both) = refs[:hops], refs[hops:]
        position, chip, core, sign = place_of()
        both[core] = mine_ref[...]
        both[1 - core] = got_ref[...]
        first, second = pair_counts(counts_ref, chip)
        for j in range(room):
            side = jnp.where(j < first, 0, 1)
            slot = jnp.minimum(j - side * first, slots - 1)
            for array in range(2):
                for hop in range(1, hops):
                    send_refs[hop - 1][array * room + j] = both[side, ((hop - 1) * 2 + array) * slots + slot]
                block = ((hops - 1) * 2 + array) * slots + slot
                home_ref[array * room + j] = both[side, block, 0:part]
                send_refs[hops - 1][array * room + j] = both[side, block, part:pair]

    return pl.pallas_call(
        kernel,
        name="pack_kinetic",
        out_shape=(
            *[VMEM((2 * room, pair, columns), jnp.float32)] * (hops - 1),
            *[VMEM((2 * room, part, columns), jnp.float32)] * 2,
        ),
        compiler_params=params(4),
        in_specs=[pl.BlockSpec(memory_space=SMEM)] + [pl.BlockSpec(memory_space=VMEM)] * 2,
        out_specs=[pl.BlockSpec(memory_space=VMEM)] * (hops + 1),
        scratch_shapes=[pltpu.VMEM((2, blocks, pair, columns), jnp.float32)],
    )(layer_counts, *near(mine, got))


def pass_rise(arrived, layer_counts, slots, room):
    _, pair, columns = arrived[0].shape
    hops = len(arrived)
    part = pair // 2

    def kernel(counts_ref, *refs):
        arrived_refs, pass_ref = refs[:hops], refs[hops]
        position, chip, core, sign = place_of()
        base = jnp.where(core == 1, 0, counts_ref[2 * chip])
        for s in range(slots):
            j = jnp.minimum(base + s, room - 1)
            for hop in range(1, hops):
                pass_ref[(hop - 1) * slots + s] = arrived_refs[hop - 1][j]
            half = s % 2 * part
            pass_ref[(hops - 1) * slots + s // 2, half : half + part] = arrived_refs[hops - 1][j]

    return pl.pallas_call(
        kernel,
        name="pass_rise",
        out_shape=VMEM(((hops - 1) * slots + slots // 2, pair, columns), jnp.float32),
        compiler_params=params(4),
        in_specs=[pl.BlockSpec(memory_space=SMEM)] + [pl.BlockSpec(memory_space=VMEM)] * hops,
        out_specs=pl.BlockSpec(memory_space=VMEM),
    )(layer_counts, *near(*arrived))


def pass_kinetic(arrived, after):
    each, pair, columns = arrived[0].shape
    part = pair // 2

    def kernel(_, *refs):
        others = pl.ds(pl.multiple_of((1 - place_of()[2]) * part, part), part)
        for i, ref in enumerate(refs[:-1]):
            refs[-1][i * each : (i + 1) * each] = ref[:, others]

    return pl.pallas_call(
        kernel,
        name="pass_kinetic",
        out_shape=VMEM((len(arrived) * each, part, columns), jnp.float32),
        compiler_params=params(4),
        in_specs=[pl.BlockSpec(memory_space=HBM)] + [pl.BlockSpec(memory_space=VMEM)] * len(arrived),
        out_specs=pl.BlockSpec(memory_space=VMEM),
    )(*far(after), *near(*arrived))


def particle(
    shell_conc, heat_rise, other_rise, arrived, passed, layer_current, layer_counts, pieces=2, chunk=64
):
    slots, shells, rows, columns = shell_conc.shape
    layers, part, _ = heat_rise.shape
    devices = layer_counts.shape[0]
    chips, hops, pair = devices // 2, len(arrived), 2 * part
    room = arrived[0].shape[0] - 1
    piece = rows // pieces
    volume = [((i + 1) ** 3 - i**3) / (3.0 * shells**3) for i in range(shells)]
    link = [DIFFUSION_STEP * ((i + 1) ** 2 / shells**2 * shells) for i in range(shells - 1)]

    def kernel(counts_ref, states_ref, current_ref, heat_ref, other_ref, passed_ref, *refs):
        arrived_refs, (out_ref, rise_ref, shell_ref, made, sem, got_sem) = refs[:hops], refs[hops:]
        fetches = [
            pltpu.make_async_copy(states_ref.at[slot], shell_ref.at[slot], got_sem.at[slot])
            for slot in range(slots)
        ]
        for fetch in fetches:
            fetch.start()
        position, chip, core, sign = place_of()
        count = counts_ref[position]
        start = lax.fori_loop(0, position, lambda d, total: total + counts_ref[d], jnp.int32(0))
        base = jnp.where(core == 0, 0, counts_ref[2 * chip])

        def rows_of(hop, begin, extent):
            first = lax.rem(chip + hop + chips, chips) * pair + begin
            return pl.ds(pl.multiple_of(first, part), extent)

        for s in range(slots):
            layer, j = jnp.minimum(start + s, layers - 1), jnp.minimum(base + s, room - 1)
            rise_ref[s, rows_of(0, core * part, part)] = heat_ref[layer]
            rise_ref[s, rows_of(0, (1 - core) * part, part)] = other_ref[layer]
            for hop in range(1, hops):
                rise_ref[s, rows_of(-sign * hop, 0, pair)] = arrived_refs[hop - 1][j]
                rise_ref[s, rows_of(sign * hop, 0, pair)] = passed_ref[(hop - 1) * slots + s]
            half = s % 2 * part
            rise_ref[s, rows_of(hops, core * part, part)] = arrived_refs[hops - 1][j]
            rise_ref[s, rows_of(hops, (1 - core) * part, part)] = passed_ref[
                (hops - 1) * slots + s // 2, half : half + part
            ]

        def solve(slot, first):
            here = slice(first, first + chunk)
            rise = rise_ref[slot, here]
            scaled = rise * (DIFFUSION_ACTIVATION / BASE_KELVIN)
            speedup = jnp.exp(scaled * reciprocal(BASE_KELVIN + rise))
            held = [None] * shells
            inverse = [None] * shells
            capacity = amount = upper = None
            for i in range(shells):
                gain = volume[i] * shell_ref[slot, i, here]
                if i == 0:
                    capacity, amount = volume[0], gain
                else:
                    capacity = volume[i] + upper * capacity
                    amount = gain + upper * amount
                if i < shells - 1:
                    flow = link[i] * speedup
                    inverse[i] = reciprocal(capacity + flow)
                    upper = flow * inverse[i]
                else:
                    amount = amount - SURFACE_STEP * current_ref[slot, here]
                    inverse[i] = reciprocal(capacity)
                held[i] = amount
            value = held[-1] * inverse[-1]
            made[slot, shells - 1, here] = value
            for i in range(shells - 2, -1, -1):
                value = inverse[i] * (held[i] + (link[i] * speedup) * value)
                made[slot, i, here] = value

        copies = []
        for slot in range(slots):
            fetches[slot].wait()
            for first in range(0, rows, piece):
                here = slice(first, first + piece)

                @pl.when(slot < count)
                def _(slot=slot, first=first):
                    for begin in range(first, first + piece, chunk):
                        solve(slot, begin)

                @pl.when(slot >= count)
                def _(slot=slot, here=here):
                    made[slot, :, here] = jnp.zeros((shells, piece, columns), jnp.float32)

                copies.append(
                    pltpu.make_async_copy(made.at[slot, :, here], out_ref.at[slot, :, here], sem.at[len(copies)])
                )
                copies[-1].start()
        for copy in copies:
            copy.wait()

    return pl.pallas_call(
        kernel,
        name="particle",
        out_shape=HBM(shell_conc.shape, jnp.float32),
        in_specs=[pl.BlockSpec(memory_space=SMEM), pl.BlockSpec(memory_space=HBM)]
        + [pl.BlockSpec(memory_space=VMEM)] * (4 + hops),
        out_specs=pl.BlockSpec(memory_space=HBM),
        scratch_shapes=[
            pltpu.VMEM((slots, rows, columns), jnp.float32),
            pltpu.VMEM(shell_conc.shape, jnp.float32),
            pltpu.VMEM(shell_conc.shape, jnp.float32),
            pltpu.SemaphoreType.DMA((slots * pieces,)),
            pltpu.SemaphoreType.DMA((slots,)),
        ],
        compiler_params=params(16),
        cost_estimate=pl.CostEstimate(
            flops=200 * slots * shells * rows * columns,
            bytes_accessed=8 * slots * shells * rows * columns,
            transcendentals=0,
        ),
    )(layer_counts, *far(shell_conc), *near(layer_current, heat_rise, other_rise, passed, *arrived))


def inverse_sine(value):
    magnitude = jnp.abs(value)
    rooted = jnp.sqrt(1.0 + magnitude * magnitude)
    positive = jnp.log1p(magnitude + magnitude * magnitude / (1.0 + rooted))
    return jnp.where(value < 0.0, -positive, positive), rooted


def column(heat_rise, other_rise, rise_edge, home, passed, arrived, faces, layer_counts, contacts):
    layers, rows, columns = heat_rise.shape
    devices = layer_counts.shape[0]
    chips, hops = devices // 2, len(arrived)
    each = home.shape[0]
    room = each // 2
    edge = rise_edge.shape[0] - 1
    last = layers - 1

    def kernel(counts_ref, contacts_ref, heat_ref, other_ref, edge_ref, faces_ref, home_ref, passed_ref, *refs):
        arrived_refs, (out_ref, place, kinetic_ref, slope_ref, right_ref) = refs[:hops], refs[hops:]
        position, chip, core, sign = place_of()
        cell = lax.axis_index("cell")
        ours = pl.ds(pl.multiple_of(core * rows, rows), rows)
        kinetic_ref[0:each] = home_ref[...]
        for hop in range(1, hops):
            kinetic_ref[hop * each : (hop + 1) * each] = arrived_refs[hop - 1][:, ours]
            back = chips - hop
            kinetic_ref[back * each : (back + 1) * each] = passed_ref[(hop - 1) * each : hop * each]
        kinetic_ref[hops * each : (hops + 1) * each] = arrived_refs[hops - 1][...]
        starts = starts_of(counts_ref, devices)
        for owner in range(chips):
            hop = lax.rem(sign * (chip - owner) + chips, chips)
            for j in range(room):
                place[starts[2 * owner] + j] = hop * each + j
        row_id = lax.broadcasted_iota(jnp.int32, (rows, columns), 0)
        lane_id = lax.broadcasted_iota(jnp.int32, (rows, columns), 1)
        for layer in range(layers):
            rise = heat_ref[layer]
            beyond = edge_ref[edge, layer : layer + 1]
            low_row = jnp.where(core == 0, beyond, other_ref[layer, rows - 1 : rows])
            high_row = jnp.where(core == 0, other_ref[layer, 0:1], beyond)
            low_row = jnp.where(position == 0, rise[0:1], low_row)
            high_row = jnp.where(position == devices - 1, rise[rows - 1 : rows], high_row)
            laplace = (
                jnp.where(row_id == 0, low_row, pltpu.roll(rise, 1, 0))
                + jnp.where(row_id == rows - 1, high_row, pltpu.roll(rise, rows - 1, 0))
                + jnp.where(lane_id == 0, rise, pltpu.roll(rise, 1, 1))
                + jnp.where(lane_id == columns - 1, rise, pltpu.roll(rise, columns - 1, 1))
                - 4.0 * rise
            )
            where = place[layer]
            surface = kinetic_ref[where]
            current = kinetic_ref[where + room]
            kelvin = BASE_KELVIN + rise
            inverse_kelvin = 1.0 / kelvin
            base_rate = (
                RATE_CONSTANT
                * jnp.exp((RATE_ACTIVATION / BASE_KELVIN) * rise * inverse_kelvin)
                * jnp.sqrt(surface * (1.0 - surface))
            )
            ratio_rate = current / (2.0 * base_rate)
            arcsine, rooted = inverse_sine(ratio_rate)
            entropic = ENTROPY_SLOPE * (0.5 - surface)
            drive = VOLT_PER_KELVIN * arcsine + entropic
            scaled = HEAT_SCALE * current
            source = scaled * (kelvin * drive)
            slope = scaled * (
                drive - (VOLT_PER_KELVIN * RATE_ACTIVATION) * ratio_rate * inverse_kelvin / rooted
            )
            right = rise + INPLANE_CONDUCT * laplace + source - slope * rise
            if layer == 0 or layer == last:
                side = 0 if layer == 0 else 1
                partner = contacts_ref[side, cell]
                face = faces_ref[jnp.maximum(partner, 0)]
                face = jnp.where(partner >= 0, face, 0.0)
                right = right + CONTACT_CONDUCT * (face - rise)
            slope_ref[layer] = slope
            right_ref[layer] = right
        upper = value = None
        for layer in range(layers):
            diagonal = 1.0 - slope_ref[layer]
            source = right_ref[layer]
            if layer > 0:
                diagonal = diagonal + THROUGH_CONDUCT - THROUGH_CONDUCT * upper
                source = source + THROUGH_CONDUCT * value
            if layer < last:
                diagonal = diagonal + THROUGH_CONDUCT
            inverse = 1.0 / diagonal
            upper = THROUGH_CONDUCT * inverse
            value = source * inverse
            slope_ref[layer] = upper
            right_ref[layer] = value
        out_ref[last] = value
        for layer in range(last - 1, -1, -1):
            value = right_ref[layer] + slope_ref[layer] * value
            out_ref[layer] = value

    return pl.pallas_call(
        kernel,
        name="column",
        out_shape=jax.ShapeDtypeStruct(heat_rise.shape, jnp.float32),
        in_specs=[pl.BlockSpec(memory_space=SMEM)] * 2 + [pl.BlockSpec(memory_space=VMEM)] * (6 + hops),
        out_specs=pl.BlockSpec(memory_space=VMEM),
        scratch_shapes=[
            pltpu.SMEM((layers + room,), jnp.int32),
            pltpu.VMEM((chips * each, rows, columns), jnp.float32),
            pltpu.VMEM((layers, rows, columns), jnp.float32),
            pltpu.VMEM((layers, rows, columns), jnp.float32),
        ],
        compiler_params=params(8),
        cost_estimate=pl.CostEstimate(
            flops=200 * layers * rows * columns, bytes_accessed=8 * layers * rows * columns, transcendentals=0
        ),
    )(layer_counts, contacts, *near(heat_rise, other_rise, rise_edge, faces, home, passed, *arrived))


def per_device(shell_conc, heat_rise, layer_current, layer_counts, contacts):
    shell_conc, heat_rise, layer_current = shell_conc[0], heat_rise[0], layer_current[0]
    slots = shell_conc.shape[0]
    layers, part, columns = heat_rise.shape
    devices = lax.axis_size("sub")
    chips = devices // 2
    room = 2 * slots
    contacts = contacts.T
    swap = [(i, i ^ 1) for i in range(devices)]
    other_rise = lax.ppermute(heat_rise, "sub", swap)
    mine, theirs = split_kinetic(shell_conc, layer_current, chips)
    got = lax.ppermute(theirs, "sub", swap)
    *send_rise, send_faces = pack_rise(heat_rise, other_rise, layer_counts, contacts, room)
    *send_kinetic, home = pack_kinetic(mine, got, layer_counts, room)
    send_rise[2:], send_kinetic = lax.optimization_barrier((send_rise[2:], send_kinetic))
    rise = [lax.ppermute(m, "sub", along(hop, chips)) for hop, m in enumerate(send_rise, 1)]
    for i, j in ((0, 2), (1, 1), (2, 0)):
        rise[i], send_kinetic[j] = lax.optimization_barrier((rise[i], send_kinetic[j]))
    kinetic = [lax.ppermute(m, "sub", along(hop, chips)) for hop, m in enumerate(send_kinetic, 1)]
    rise[3], send_faces = lax.optimization_barrier((rise[3], send_faces))
    faces = lax.all_to_all(send_faces, "cell", 0, 0, tiled=True)
    passed_rise = lax.ppermute(pass_rise(rise, layer_counts, slots, room), "sub", swap)
    conc_new = particle(shell_conc, heat_rise, other_rise, rise, passed_rise, layer_current, layer_counts)
    kinetic, faces = lax.optimization_barrier((kinetic, faces))
    passed_kinetic = lax.ppermute(pass_kinetic(kinetic[:-1], conc_new), "sub", swap)
    heat_new = column(
        heat_rise, other_rise, rise[0], home, passed_kinetic, kinetic, faces, layer_counts, contacts
    )
    return conc_new[None], heat_new[None]


def solution(mesh):
    in_specs = (
        P("cell", "sub", None, None, None),
        P("cell", None, "sub", None),
        P("cell", "sub", None, None),
        P(),
        P(),
    )
    out_specs = (P("cell", "sub", None, None, None), P("cell", None, "sub", None))
    return jax.shard_map(
        per_device, mesh=mesh, in_specs=in_specs, out_specs=out_specs, check_vma=False
    )
```

time: 57.8 us -> 55.2 us (0.955)
  the two profiles are of different devices: /device:TPU:2 before, /device:TPU:1 now
where the time goes in v3:
time: 55.2 us; the launch traced here: 55 us
  starting transfers between devices  37.3 us (68%)
  Pallas kernels  12.2 us (22%)
  waiting for transfers between devices  4.73 us (9%)
  between operations  0.74 us (1%)
    ppermute x8, starting transfers between devices, per_device(): lax.ppermute(m, 'sub', along(hop, chips))  19.3 us
    all_to_all x1, starting transfers between devices, per_device(): faces = lax.all_to_all(send_faces, 'cell', 0, 0, tiled=True)  6.78 us
    ppermute x1, starting transfers between devices, per_device(): lax.ppermute(pass_kinetic(kinetic[:-1], conc_new), 'sub', swap)  5.39 us
    pallas_call x1, Pallas kernels, particle(): pl.pallas_call(kernel, name='particle', out_shape=HBM(shell_conc.shape, j...  5.08 us
    ppermute x1, starting transfers between devices, per_device(): got = lax.ppermute(theirs, 'sub', swap)  3.33 us
    ppermute x1, starting transfers between devices, per_device(): lax.ppermute(pass_rise(rise, layer_counts, slots, room), 'sub', swap)  2.42 us
    pallas_call x1, Pallas kernels, column(): pl.pallas_call(kernel, name='column', out_shape=jax.ShapeDtypeStruct(heat...  2.18 us
    ppermute x1, waiting for transfers between devices, per_device(): other_rise = lax.ppermute(heat_rise, 'sub', swap)  1.78 us
  transfers between devices with their start and end apart: 13, of which 3 were waited for; matrix products, arithmetic and copies ran while one was open for 0% of the time, Pallas kernels for 15%

profile of v3, /device:TPU:1, one launch (start us, length us, event | category | flops | bytes accessed | tf_op | source)
XLA Modules:
  0.0 55.0 jit_solution(15007128893379888625)
XLA Ops:
  0.6 0.0 copy-start.1
  0.6 0.0 copy-start
  0.7 0.0 copy-start.2
  0.7 0.0 copy-start.3
  0.7 1.5 %split_kinetic.1 = (f32[32,32,128]{2,1,0:T(8,128)S(1)}, f32[32,32,128]{2,1,0:T(8,128)S(1)}) custom-call(f32[4,10,256,128]{3,2,1,0:T(8,128)} %bitcast.14, f32[4,256,128]{2,1,0:T(8,128)} %bitcast.10), custom_call_target="tpu_custom_call" | custom-call | tf_op jit(solution)/shard_map/split_kinetic/pallas_call | solution.py:99
  2.2 3.3 %collective-permute-start.2 = (f32[32,32,128]{2,1,0:T(8,128)S(1)}, f32[32,32,128]{2,1,0:T(8,128)S(1)}, u32[]{:S(2)}, u32[]{:S(2)}) collective-permute-start(f32[32,32,128]{2,1,0:T(8,128)S(1)} %get-tuple-element.37), channel_id=1, source_target_pairs={{0,1},{1,0},{2,3},{3,2},{4,5},{5,4},{6,7},{7,6},{8,9},{9,8},{10,11... | collective-permute-start | bytes 1572872 | tf_op jit(solution)/shard_map/ppermute | solution.py:479
  5.5 0.0 copy-done
  5.5 0.1 collective-permute-start
  5.6 1.8 %collective-permute-done.other_ref = f32[30,16,128]{2,1,0:T(8,128)S(1)} collective-permute-done((f32[30,16,128]{2,1,0:T(8,128)S(1)}, f32[30,16,128]{2,1,0:T(8,128)S(1)}, u32[]{:S(2)}, u32[]{:S(2)}) %collective-permute-start) | collective-permute-done | bytes 245792 | tf_op jit(solution)/shard_map/ppermute | solution.py:477
  7.4 0.0 copy-done.2
  7.4 0.0 copy-done.3
  7.4 1.3 %pack_rise.1 = (f32[9,32,128]{2,1,0:T(8,128)S(1)}, f32[8,32,128]{2,1,0:T(8,128)S(1)}, f32[8,32,128]{2,1,0:T(8,128)S(1)}, f32[8,16,128]{2,1,0:T(8,128)S(1)}, f32[16,16,128]{2,1,0:T(8,128)}) custom-call(s32[16]{0:T(128)S(1)} %copy-done.2, s32[2,16]{1,0:T(2,128)S(1)} %bitcast.12, f32[30,16,128]{2,1,0:T(8,128)S(1)} %bitcast.7, ...), custom_call_target="tpu_custom_call" | custom-call | tf_op jit(solution)/shard_map/pack_rise/pallas_call | solution.py:141
  8.7 3.8 %collective-permute-start.1 = (f32[9,32,128]{2,1,0:T(8,128)S(1)}, f32[9,32,128]{2,1,0:T(8,128)S(1)}, u32[]{:S(2)}, u32[]{:S(2)}) collective-permute-start(f32[9,32,128]{2,1,0:T(8,128)S(1)} %get-tuple-element.33), channel_id=1, source_target_pairs={{0,2},{1,15},{2,4},{3,1},{4,6},{5,3},{6,8},{7,5},{8,10},{9,7},{10,... | collective-permute-start | bytes 442376 | tf_op jit(solution)/shard_map/ppermute | solution.py:483
  12.5 1.2 %collective-permute-start.3 = (f32[8,32,128]{2,1,0:T(8,128)S(1)}, f32[8,32,128]{2,1,0:T(8,128)S(1)}, u32[]{:S(2)}, u32[]{:S(2)}) collective-permute-start(f32[8,32,128]{2,1,0:T(8,128)S(1)} %get-tuple-element.44), channel_id=1, source_target_pairs={{0,4},{1,13},{2,6},{3,15},{4,8},{5,1},{6,10},{7,3},{8,12},{9,5},{1... | collective-permute-start | bytes 393224 | tf_op jit(solution)/shard_map/ppermute | solution.py:483
  13.7 0.0 collective-permute-done.2.got_ref
  13.7 1.5 %pack_kinetic.1 = (f32[16,32,128]{2,1,0:T(8,128)S(1)}, f32[16,32,128]{2,1,0:T(8,128)}, f32[16,32,128]{2,1,0:T(8,128)}, f32[16,16,128]{2,1,0:T(8,128)S(1)}, f32[16,16,128]{2,1,0:T(8,128)S(1)}) custom-call(s32[16]{0:T(128)S(1)} %copy-done.2, f32[32,32,128]{2,1,0:T(8,128)S(1)} %get-tuple-element.36.mine_ref, f32[32,32,128]{2,1,0:T(8,128)S(1)} %collective-permute-done.2.got_ref), custom_call_target="tpu_custom_call" | custom-call | tf_op jit(solution)/shard_map/pack_kinetic/pallas_call | solution.py:179
  15.2 0.4 collective-permute-start.4
  15.7 4.5 %collective-permute-start.5 = (f32[8,16,128]{2,1,0:T(8,128)S(1)}, f32[8,16,128]{2,1,0:T(8,128)S(1)}, u32[]{:S(2)}, u32[]{:S(2)}) collective-permute-start(f32[8,16,128]{2,1,0:T(8,128)S(1)} %get-tuple-element.50), channel_id=1, source_target_pairs={{0,8},{1,9},{2,10},{3,11},{4,12},{5,13},{6,14},{7,15},{8,0},{9,1},... | collective-permute-start | bytes 196616 | tf_op jit(solution)/shard_map/ppermute | solution.py:483
  20.1 0.0 collective-permute-done.1.refs_0_.edge_ref
  20.1 0.0 collective-permute-done.3.refs_1_
  20.1 1.2 %collective-permute-start.8 = (f32[16,32,128]{2,1,0:T(8,128)}, f32[16,32,128]{2,1,0:T(8,128)S(1)}, u32[]{:S(2)}, u32[]{:S(2)}) collective-permute-start(f32[16,32,128]{2,1,0:T(8,128)} %get-tuple-element.54), channel_id=1, source_target_pairs={{0,4},{1,13},{2,6},{3,15},{4,8},{5,1},{6,10},{7,3},{8,12},{9,5},{1... | collective-permute-start | bytes 786440 | tf_op jit(solution)/shard_map/ppermute | solution.py:486
  21.3 0.9 %collective-permute-start.9 = (f32[16,32,128]{2,1,0:T(8,128)}, f32[16,32,128]{2,1,0:T(8,128)S(1)}, u32[]{:S(2)}, u32[]{:S(2)}) collective-permute-start(f32[16,32,128]{2,1,0:T(8,128)} %get-tuple-element.55), channel_id=1, source_target_pairs={{0,6},{1,11},{2,8},{3,13},{4,10},{5,15},{6,12},{7,1},{8,14},{9,3},... | collective-permute-start | bytes 786440 | tf_op jit(solution)/shard_map/ppermute | solution.py:486
  22.2 0.0 collective-permute-done.4.refs_2_
  22.2 4.0 %collective-permute-start.7 = (f32[16,32,128]{2,1,0:T(8,128)S(1)}, f32[16,32,128]{2,1,0:T(8,128)S(1)}, u32[]{:S(2)}, u32[]{:S(2)}) collective-permute-start(f32[16,32,128]{2,1,0:T(8,128)S(1)} %get-tuple-element.53), channel_id=1, source_target_pairs={{0,2},{1,15},{2,4},{3,1},{4,6},{5,3},{6,8},{7,5},{8,10},{9,7},{10,... | collective-permute-start | bytes 786440 | tf_op jit(solution)/shard_map/ppermute | solution.py:486
  26.2 0.0 collective-permute-done.5.refs_3_
  26.2 0.6 %pass_rise.1 = f32[14,32,128]{2,1,0:T(8,128)S(1)} custom-call(s32[16]{0:T(128)S(1)} %copy-done.2, f32[9,32,128]{2,1,0:T(8,128)S(1)} %collective-permute-done.1.refs_0_.edge_ref, f32[8,32,128]{2,1,0:T(8,128)S(1)} %collective-permute-done.3.refs_1_, f32[8,32,128]{2,1,0:T(8,128)S(1)} %collective-permute-done.4.refs_2_, ...), custom_call_target="tpu_custom_call" | custom-call | tf_op jit(solution)/shard_map/pass_rise/pallas_call | solution.py:209
  26.8 2.4 %collective-permute-start.6 = (f32[14,32,128]{2,1,0:T(8,128)S(1)}, f32[14,32,128]{2,1,0:T(8,128)S(1)}, u32[]{:S(2)}, u32[]{:S(2)}) collective-permute-start(f32[14,32,128]{2,1,0:T(8,128)S(1)} %pass_rise.1), channel_id=1, source_target_pairs={{0,1},{1,0},{2,3},{3,2},{4,5},{5,4},{6,7},{7,6},{8,9},{9,8},{10,11... | collective-permute-start | bytes 688136 | tf_op jit(solution)/shard_map/ppermute | solution.py:489
  29.2 3.3 %collective-permute-start.10 = (f32[16,16,128]{2,1,0:T(8,128)S(1)}, f32[16,16,128]{2,1,0:T(8,128)S(1)}, u32[]{:S(2)}, u32[]{:S(2)}) collective-permute-start(f32[16,16,128]{2,1,0:T(8,128)S(1)} %get-tuple-element.56), channel_id=1, source_target_pairs={{0,8},{1,9},{2,10},{3,11},{4,12},{5,13},{6,14},{7,15},{8,0},{9,1},... | collective-permute-start | bytes 393224 | tf_op jit(solution)/shard_map/ppermute | solution.py:486
  32.5 6.8 %all-to-all-start = ((f32[16,16,128]{2,1,0:T(8,128)}), f32[16,16,128]{2,1,0:T(8,128)S(1)}, u32[]{:S(2)}, u32[]{:S(2)}) async-start(f32[16,16,128]{2,1,0:T(8,128)} %get-tuple-element.57), calls=%async_computation | async-start | bytes 262144 | tf_op jit(solution)/shard_map/all_to_all | solution.py:488
  39.3 0.0 collective-permute-done.6.passed_ref
  39.3 0.0 copy-done.1
  39.3 5.1 %particle.1._ = f32[4,10,256,128]{3,2,1,0:T(8,128)} custom-call(s32[16]{0:T(128)S(1)} %copy-done.2, f32[4,10,256,128]{3,2,1,0:T(8,128)} %bitcast.15, f32[4,256,128]{2,1,0:T(8,128)S(1)} %bitcast.11, f32[30,16,128]{2,1,0:T(8,128)S(1)} %bitcast.8, f32[30,16,128]{2,1,0:T(8,128)S(1)} %collective-permute-done.other_ref, ...), custom_call_target="tpu_custom_call" | custom-call | flops 262144000 | bytes 10485760 | tf_op jit(solution)/shard_map/particle/pallas_call | solution.py:331
  44.4 0.0 collective-permute-done.10.refs_3_
  44.4 1.6 %all-to-all-done.faces_ref = f32[16,16,128]{2,1,0:T(8,128)S(1)} async-done(((f32[16,16,128]{2,1,0:T(8,128)}), f32[16,16,128]{2,1,0:T(8,128)S(1)}, u32[]{:S(2)}, u32[]{:S(2)}) %all-to-all-start) | async-done | bytes 131104 | tf_op jit(solution)/shard_map/all_to_all | solution.py:488
  46.0 0.0 collective-permute-done.8.refs_1_
  46.0 0.0 collective-permute-done.9.refs_2_
  46.0 0.0 collective-permute-done.7.refs_0_
  46.0 5.4 %collective-permute-start.11 = (f32[48,16,128]{2,1,0:T(8,128)S(1)}, f32[48,16,128]{2,1,0:T(8,128)S(1)}, u32[]{:S(2)}, u32[]{:S(2)}) collective-permute-start(f32[48,16,128]{2,1,0:T(8,128)S(1)} %pass_kinetic.1), channel_id=1, source_target_pairs={{0,1},{1,0},{2,3},{3,2},{4,5},{5,4},{6,7},{7,6},{8,9},{9,8},{10,11... | collective-permute-start | bytes 1179656 | tf_op jit(solution)/shard_map/ppermute | solution.py:492
  51.4 1.3 %collective-permute-done.11.passed_ref = f32[48,16,128]{2,1,0:T(8,128)S(1)} collective-permute-done((f32[48,16,128]{2,1,0:T(8,128)S(1)}, f32[48,16,128]{2,1,0:T(8,128)S(1)}, u32[]{:S(2)}, u32[]{:S(2)}) %collective-permute-start.11) | collective-permute-done | bytes 393248 | tf_op jit(solution)/shard_map/ppermute | solution.py:492
  52.8 2.2 %column.1 = f32[30,16,128]{2,1,0:T(8,128)} custom-call(s32[16]{0:T(128)S(1)} %copy-done.2, s32[2,16]{1,0:T(2,128)S(1)} %bitcast.13, f32[30,16,128]{2,1,0:T(8,128)S(1)} %bitcast.9, f32[30,16,128]{2,1,0:T(8,128)S(1)} %collective-permute-done.other_ref, f32[9,32,128]{2,1,0:T(8,128)S(1)} %collective-permute-done.1.refs_0_.edge_ref, ...), custom_call_target="tpu_custom_call" | custom-call | flops 12288000 | bytes 491520 | tf_op jit(solution)/shard_map/column/pallas_call | solution.py:449
  (1 shorter events, 0.0 us)
Async XLA Ops:
  0.6 38.7 %copy-start.1 = (f32[1,4,256,128]{3,2,1,0:T(8,128)S(1)}, f32[1,4,256,128]{3,2,1,0:T(8,128)}, u32[]{:S(2)}) copy-start(f32[1,4,256,128]{3,2,1,0:T(8,128)} %param.7) | copy-start | bytes 1572868
  0.6 4.8 %copy-start = (f32[1,30,16,128]{3,2,1,0:T(8,128)S(1)}, f32[1,30,16,128]{3,2,1,0:T(8,128)}, u32[]{:S(2)}) copy-start(f32[1,30,16,128]{3,2,1,0:T(8,128)} %param.6) | copy-start | bytes 737284
  0.7 6.7 %copy-start.2 = (s32[16]{0:T(128)S(1)}, s32[16]{0:T(128)}, u32[]{:S(2)}) copy-start(s32[16]{0:T(128)} %counts_ref.9) | copy-start | bytes 196
  0.7 6.7 %copy-start.3 = (s32[16,2]{0,1:T(2,128)S(1)}, s32[16,2]{0,1:T(2,128)}, u32[]{:S(2)}) copy-start(s32[16,2]{0,1:T(2,128)} %param.9) | copy-start | bytes 388
  2.2 11.6 %collective-permute-start.2 = (f32[32,32,128]{2,1,0:T(8,128)S(1)}, f32[32,32,128]{2,1,0:T(8,128)S(1)}, u32[]{:S(2)}, u32[]{:S(2)}) collective-permute-start(f32[32,32,128]{2,1,0:T(8,128)S(1)} %get-tuple-element.37), channel_id=1, source_target_pairs={{0,1},{1,0},{2,3},{3,2},{4,5},{5,4},{6,7},{7,6},{8,9},{9,8},{10,11... | collective-permute-start | bytes 1572872 | tf_op jit(solution)/shard_map/ppermute | solution.py:479
  5.5 1.9 %collective-permute-start = (f32[30,16,128]{2,1,0:T(8,128)S(1)}, f32[30,16,128]{2,1,0:T(8,128)S(1)}, u32[]{:S(2)}, u32[]{:S(2)}) collective-permute-start(f32[30,16,128]{2,1,0:T(8,128)S(1)} %bitcast.6), channel_id=1, source_target_pairs={{0,1},{1,0},{2,3},{3,2},{4,5},{5,4},{6,7},{7,6},{8,9},{9,8},{10,11... | collective-permute-start | bytes 737288 | tf_op jit(solution)/shard_map/ppermute | solution.py:477
  8.7 11.4 %collective-permute-start.1 = (f32[9,32,128]{2,1,0:T(8,128)S(1)}, f32[9,32,128]{2,1,0:T(8,128)S(1)}, u32[]{:S(2)}, u32[]{:S(2)}) collective-permute-start(f32[9,32,128]{2,1,0:T(8,128)S(1)} %get-tuple-element.33), channel_id=1, source_target_pairs={{0,2},{1,15},{2,4},{3,1},{4,6},{5,3},{6,8},{7,5},{8,10},{9,7},{10,... | collective-permute-start | bytes 442376 | tf_op jit(solution)/shard_map/ppermute | solution.py:483
  12.5 7.6 %collective-permute-start.3 = (f32[8,32,128]{2,1,0:T(8,128)S(1)}, f32[8,32,128]{2,1,0:T(8,128)S(1)}, u32[]{:S(2)}, u32[]{:S(2)}) collective-permute-start(f32[8,32,128]{2,1,0:T(8,128)S(1)} %get-tuple-element.44), channel_id=1, source_target_pairs={{0,4},{1,13},{2,6},{3,15},{4,8},{5,1},{6,10},{7,3},{8,12},{9,5},{1... | collective-permute-start | bytes 393224 | tf_op jit(solution)/shard_map/ppermute | solution.py:483
  15.2 7.0 %collective-permute-start.4 = (f32[8,32,128]{2,1,0:T(8,128)S(1)}, f32[8,32,128]{2,1,0:T(8,128)S(1)}, u32[]{:S(2)}, u32[]{:S(2)}) collective-permute-start(f32[8,32,128]{2,1,0:T(8,128)S(1)} %get-tuple-element.47), channel_id=1, source_target_pairs={{0,6},{1,11},{2,8},{3,13},{4,10},{5,15},{6,12},{7,1},{8,14},{9,3},... | collective-permute-start | bytes 393224 | tf_op jit(solution)/shard_map/ppermute | solution.py:483
  15.7 10.5 %collective-permute-start.5 = (f32[8,16,128]{2,1,0:T(8,128)S(1)}, f32[8,16,128]{2,1,0:T(8,128)S(1)}, u32[]{:S(2)}, u32[]{:S(2)}) collective-permute-start(f32[8,16,128]{2,1,0:T(8,128)S(1)} %get-tuple-element.50), channel_id=1, source_target_pairs={{0,8},{1,9},{2,10},{3,11},{4,12},{5,13},{6,14},{7,15},{8,0},{9,1},... | collective-permute-start | bytes 196616 | tf_op jit(solution)/shard_map/ppermute | solution.py:483
  20.1 25.8 %collective-permute-start.8 = (f32[16,32,128]{2,1,0:T(8,128)}, f32[16,32,128]{2,1,0:T(8,128)S(1)}, u32[]{:S(2)}, u32[]{:S(2)}) collective-permute-start(f32[16,32,128]{2,1,0:T(8,128)} %get-tuple-element.54), channel_id=1, source_target_pairs={{0,4},{1,13},{2,6},{3,15},{4,8},{5,1},{6,10},{7,3},{8,12},{9,5},{1... | collective-permute-start | bytes 786440 | tf_op jit(solution)/shard_map/ppermute | solution.py:486
  21.3 24.7 %collective-permute-start.9 = (f32[16,32,128]{2,1,0:T(8,128)}, f32[16,32,128]{2,1,0:T(8,128)S(1)}, u32[]{:S(2)}, u32[]{:S(2)}) collective-permute-start(f32[16,32,128]{2,1,0:T(8,128)} %get-tuple-element.55), channel_id=1, source_target_pairs={{0,6},{1,11},{2,8},{3,13},{4,10},{5,15},{6,12},{7,1},{8,14},{9,3},... | collective-permute-start | bytes 786440 | tf_op jit(solution)/shard_map/ppermute | solution.py:486
  22.2 23.8 %collective-permute-start.7 = (f32[16,32,128]{2,1,0:T(8,128)S(1)}, f32[16,32,128]{2,1,0:T(8,128)S(1)}, u32[]{:S(2)}, u32[]{:S(2)}) collective-permute-start(f32[16,32,128]{2,1,0:T(8,128)S(1)} %get-tuple-element.53), channel_id=1, source_target_pairs={{0,2},{1,15},{2,4},{3,1},{4,6},{5,3},{6,8},{7,5},{8,10},{9,7},{10,... | collective-permute-start | bytes 786440 | tf_op jit(solution)/shard_map/ppermute | solution.py:486
  26.8 12.5 %collective-permute-start.6 = (f32[14,32,128]{2,1,0:T(8,128)S(1)}, f32[14,32,128]{2,1,0:T(8,128)S(1)}, u32[]{:S(2)}, u32[]{:S(2)}) collective-permute-start(f32[14,32,128]{2,1,0:T(8,128)S(1)} %pass_rise.1), channel_id=1, source_target_pairs={{0,1},{1,0},{2,3},{3,2},{4,5},{5,4},{6,7},{7,6},{8,9},{9,8},{10,11... | collective-permute-start | bytes 688136 | tf_op jit(solution)/shard_map/ppermute | solution.py:489
  29.2 15.2 %collective-permute-start.10 = (f32[16,16,128]{2,1,0:T(8,128)S(1)}, f32[16,16,128]{2,1,0:T(8,128)S(1)}, u32[]{:S(2)}, u32[]{:S(2)}) collective-permute-start(f32[16,16,128]{2,1,0:T(8,128)S(1)} %get-tuple-element.56), channel_id=1, source_target_pairs={{0,8},{1,9},{2,10},{3,11},{4,12},{5,13},{6,14},{7,15},{8,0},{9,1},... | collective-permute-start | bytes 393224 | tf_op jit(solution)/shard_map/ppermute | solution.py:486
  32.5 13.5 %all-to-all-start = ((f32[16,16,128]{2,1,0:T(8,128)}), f32[16,16,128]{2,1,0:T(8,128)S(1)}, u32[]{:S(2)}, u32[]{:S(2)}) async-start(f32[16,16,128]{2,1,0:T(8,128)} %get-tuple-element.57), calls=%async_computation | async-start | bytes 262144 | tf_op jit(solution)/shard_map/all_to_all | solution.py:488
  46.0 6.7 %collective-permute-start.11 = (f32[48,16,128]{2,1,0:T(8,128)S(1)}, f32[48,16,128]{2,1,0:T(8,128)S(1)}, u32[]{:S(2)}, u32[]{:S(2)}) collective-permute-start(f32[48,16,128]{2,1,0:T(8,128)S(1)} %pass_kinetic.1), channel_id=1, source_target_pairs={{0,1},{1,0},{2,3},{3,2},{4,5},{5,4},{6,7},{7,6},{8,9},{9,8},{10,11... | collective-permute-start | bytes 1179656 | tf_op jit(solution)/shard_map/ppermute | solution.py:492

commit v4 on v3

--- a/solution.py
+++ b/solution.py
@@ -475,7 +475,8 @@
     contacts = contacts.T
     swap = [(i, i ^ 1) for i in range(devices)]
     other_rise = lax.ppermute(heat_rise, "sub", swap)
-    mine, theirs = split_kinetic(shell_conc, layer_current, chips)
+    other_rise, current = lax.optimization_barrier((other_rise, layer_current))
+    mine, theirs = split_kinetic(shell_conc, current, chips)
     got = lax.ppermute(theirs, "sub", swap)
     *send_rise, send_faces = pack_rise(heat_rise, other_rise, layer_counts, contacts, room)
     *send_kinetic, home = pack_kinetic(mine, got, layer_counts, room)

time: 55.2 us -> 54.8 us (level)
    ppermute x1, starting transfers between devices: 0.11 us -> 3.33 us  [per_device(): other_rise = lax.ppermute(heat_rise, 'sub', swap)]
    ppermute x1, starting transfers between devices: 3.33 us -> 0.46 us  [per_device(): got = lax.ppermute(theirs, 'sub', swap)]
where the time goes in v4:
time: 54.8 us; the launch traced here: 54.6 us
  starting transfers between devices  37.5 us (68%)
  Pallas kernels  12.1 us (22%)
  waiting for transfers between devices  4.3 us (8%)
  between operations  0.74 us (1%)
    ppermute x8, starting transfers between devices, per_device(): lax.ppermute(m, 'sub', along(hop, chips))  19.3 us
    all_to_all x1, starting transfers between devices, per_device(): faces = lax.all_to_all(send_faces, 'cell', 0, 0, tiled=True)  6.78 us
    ppermute x1, starting transfers between devices, per_device(): lax.ppermute(pass_kinetic(kinetic[:-1], conc_new), 'sub', swap)  5.39 us
    pallas_call x1, Pallas kernels, particle(): pl.pallas_call(kernel, name='particle', out_shape=HBM(shell_conc.shape, j...  5.08 us
    ppermute x1, starting transfers between devices, per_device(): other_rise = lax.ppermute(heat_rise, 'sub', swap)  3.33 us
    pallas_call x1, Pallas kernels, column(): pl.pallas_call(kernel, name='column', out_shape=jax.ShapeDtypeStruct(heat...  2.18 us
    ppermute x1, starting transfers between devices, per_device(): lax.ppermute(pass_rise(rise, layer_counts, slots, room), 'sub', swap)  2.17 us
    all_to_all x1, waiting for transfers between devices, per_device(): faces = lax.all_to_all(send_faces, 'cell', 0, 0, tiled=True)  1.58 us
  transfers between devices with their start and end apart: 13, of which 3 were waited for; matrix products, arithmetic and copies ran while one was open for 0% of the time, Pallas kernels for 15%

profile of v4, /device:TPU:1, one launch (start us, length us, event | category | flops | bytes accessed | tf_op | source)
XLA Modules:
  0.0 54.6 jit_solution(1462848378933793771)
XLA Ops:
  0.6 0.0 copy-start
  0.6 0.0 copy-start.1
  0.7 0.0 copy-start.2
  0.7 0.0 copy-start.3
  0.7 3.3 %collective-permute-start = (f32[30,16,128]{2,1,0:T(8,128)}, f32[30,16,128]{2,1,0:T(8,128)S(1)}, u32[]{:S(2)}, u32[]{:S(2)}) collective-permute-start(f32[30,16,128]{2,1,0:T(8,128)} %bitcast.6), channel_id=1, source_target_pairs={{0,1},{1,0},{2,3},{3,2},{4,5},{5,4},{6,7},{7,6},{8,9},{9,8},{10,11... | collective-permute-start | bytes 737288 | tf_op jit(solution)/shard_map/ppermute | solution.py:477
  4.0 1.3 %collective-permute-done.other_ref = f32[30,16,128]{2,1,0:T(8,128)S(1)} collective-permute-done((f32[30,16,128]{2,1,0:T(8,128)}, f32[30,16,128]{2,1,0:T(8,128)S(1)}, u32[]{:S(2)}, u32[]{:S(2)}) %collective-permute-start) | collective-permute-done | bytes 245792 | tf_op jit(solution)/shard_map/ppermute | solution.py:477
  5.3 1.4 %split_kinetic.1 = (f32[32,32,128]{2,1,0:T(8,128)S(1)}, f32[32,32,128]{2,1,0:T(8,128)S(1)}) custom-call(f32[4,10,256,128]{3,2,1,0:T(8,128)} %bitcast.14, f32[4,256,128]{2,1,0:T(8,128)} %bitcast.10), custom_call_target="tpu_custom_call" | custom-call | tf_op jit(solution)/shard_map/split_kinetic/pallas_call | solution.py:99
  6.8 0.5 collective-permute-start.2
  7.2 0.0 copy-done
  7.2 0.0 copy-done.2
  7.2 0.0 copy-done.3
  7.2 1.3 %pack_rise.1 = (f32[9,32,128]{2,1,0:T(8,128)S(1)}, f32[8,32,128]{2,1,0:T(8,128)S(1)}, f32[8,32,128]{2,1,0:T(8,128)S(1)}, f32[8,16,128]{2,1,0:T(8,128)S(1)}, f32[16,16,128]{2,1,0:T(8,128)}) custom-call(s32[16]{0:T(128)S(1)} %copy-done.2, s32[2,16]{1,0:T(2,128)S(1)} %bitcast.12, f32[30,16,128]{2,1,0:T(8,128)S(1)} %bitcast.7, ...), custom_call_target="tpu_custom_call" | custom-call | tf_op jit(solution)/shard_map/pack_rise/pallas_call | solution.py:141
  8.5 3.8 %collective-permute-start.1 = (f32[9,32,128]{2,1,0:T(8,128)S(1)}, f32[9,32,128]{2,1,0:T(8,128)S(1)}, u32[]{:S(2)}, u32[]{:S(2)}) collective-permute-start(f32[9,32,128]{2,1,0:T(8,128)S(1)} %get-tuple-element.36), channel_id=1, source_target_pairs={{0,2},{1,15},{2,4},{3,1},{4,6},{5,3},{6,8},{7,5},{8,10},{9,7},{10,... | collective-permute-start | bytes 442376 | tf_op jit(solution)/shard_map/ppermute | solution.py:484
  12.4 1.2 %collective-permute-start.3 = (f32[8,32,128]{2,1,0:T(8,128)S(1)}, f32[8,32,128]{2,1,0:T(8,128)S(1)}, u32[]{:S(2)}, u32[]{:S(2)}) collective-permute-start(f32[8,32,128]{2,1,0:T(8,128)S(1)} %get-tuple-element.48), channel_id=1, source_target_pairs={{0,4},{1,13},{2,6},{3,15},{4,8},{5,1},{6,10},{7,3},{8,12},{9,5},{1... | collective-permute-start | bytes 393224 | tf_op jit(solution)/shard_map/ppermute | solution.py:484
  13.6 0.0 collective-permute-done.2.got_ref
  13.6 1.5 %pack_kinetic.1 = (f32[16,32,128]{2,1,0:T(8,128)S(1)}, f32[16,32,128]{2,1,0:T(8,128)}, f32[16,32,128]{2,1,0:T(8,128)}, f32[16,16,128]{2,1,0:T(8,128)S(1)}, f32[16,16,128]{2,1,0:T(8,128)S(1)}) custom-call(s32[16]{0:T(128)S(1)} %copy-done.2, f32[32,32,128]{2,1,0:T(8,128)S(1)} %get-tuple-element.40.mine_ref, f32[32,32,128]{2,1,0:T(8,128)S(1)} %collective-permute-done.2.got_ref), custom_call_target="tpu_custom_call" | custom-call | tf_op jit(solution)/shard_map/pack_kinetic/pallas_call | solution.py:179
  15.0 0.4 collective-permute-start.4
  15.5 4.5 %collective-permute-start.5 = (f32[8,16,128]{2,1,0:T(8,128)S(1)}, f32[8,16,128]{2,1,0:T(8,128)S(1)}, u32[]{:S(2)}, u32[]{:S(2)}) collective-permute-start(f32[8,16,128]{2,1,0:T(8,128)S(1)} %get-tuple-element.54), channel_id=1, source_target_pairs={{0,8},{1,9},{2,10},{3,11},{4,12},{5,13},{6,14},{7,15},{8,0},{9,1},... | collective-permute-start | bytes 196616 | tf_op jit(solution)/shard_map/ppermute | solution.py:484
  20.0 0.0 collective-permute-done.1.refs_0_.edge_ref
  20.0 0.0 collective-permute-done.3.refs_1_
  20.0 1.2 %collective-permute-start.8 = (f32[16,32,128]{2,1,0:T(8,128)}, f32[16,32,128]{2,1,0:T(8,128)S(1)}, u32[]{:S(2)}, u32[]{:S(2)}) collective-permute-start(f32[16,32,128]{2,1,0:T(8,128)} %get-tuple-element.58), channel_id=1, source_target_pairs={{0,4},{1,13},{2,6},{3,15},{4,8},{5,1},{6,10},{7,3},{8,12},{9,5},{1... | collective-permute-start | bytes 786440 | tf_op jit(solution)/shard_map/ppermute | solution.py:487
  21.2 0.9 %collective-permute-start.9 = (f32[16,32,128]{2,1,0:T(8,128)}, f32[16,32,128]{2,1,0:T(8,128)S(1)}, u32[]{:S(2)}, u32[]{:S(2)}) collective-permute-start(f32[16,32,128]{2,1,0:T(8,128)} %get-tuple-element.59), channel_id=1, source_target_pairs={{0,6},{1,11},{2,8},{3,13},{4,10},{5,15},{6,12},{7,1},{8,14},{9,3},... | collective-permute-start | bytes 786440 | tf_op jit(solution)/shard_map/ppermute | solution.py:487
  22.1 0.0 collective-permute-done.4.refs_2_
  22.1 4.0 %collective-permute-start.7 = (f32[16,32,128]{2,1,0:T(8,128)S(1)}, f32[16,32,128]{2,1,0:T(8,128)S(1)}, u32[]{:S(2)}, u32[]{:S(2)}) collective-permute-start(f32[16,32,128]{2,1,0:T(8,128)S(1)} %get-tuple-element.57), channel_id=1, source_target_pairs={{0,2},{1,15},{2,4},{3,1},{4,6},{5,3},{6,8},{7,5},{8,10},{9,7},{10,... | collective-permute-start | bytes 786440 | tf_op jit(solution)/shard_map/ppermute | solution.py:487
  26.0 0.0 collective-permute-done.5.refs_3_
  26.0 0.6 %pass_rise.1 = f32[14,32,128]{2,1,0:T(8,128)S(1)} custom-call(s32[16]{0:T(128)S(1)} %copy-done.2, f32[9,32,128]{2,1,0:T(8,128)S(1)} %collective-permute-done.1.refs_0_.edge_ref, f32[8,32,128]{2,1,0:T(8,128)S(1)} %collective-permute-done.3.refs_1_, f32[8,32,128]{2,1,0:T(8,128)S(1)} %collective-permute-done.4.refs_2_, ...), custom_call_target="tpu_custom_call" | custom-call | tf_op jit(solution)/shard_map/pass_rise/pallas_call | solution.py:209
  26.6 2.2 %collective-permute-start.6 = (f32[14,32,128]{2,1,0:T(8,128)S(1)}, f32[14,32,128]{2,1,0:T(8,128)S(1)}, u32[]{:S(2)}, u32[]{:S(2)}) collective-permute-start(f32[14,32,128]{2,1,0:T(8,128)S(1)} %pass_rise.1), channel_id=1, source_target_pairs={{0,1},{1,0},{2,3},{3,2},{4,5},{5,4},{6,7},{7,6},{8,9},{9,8},{10,11... | collective-permute-start | bytes 688136 | tf_op jit(solution)/shard_map/ppermute | solution.py:490
  28.8 3.4 %collective-permute-start.10 = (f32[16,16,128]{2,1,0:T(8,128)S(1)}, f32[16,16,128]{2,1,0:T(8,128)S(1)}, u32[]{:S(2)}, u32[]{:S(2)}) collective-permute-start(f32[16,16,128]{2,1,0:T(8,128)S(1)} %get-tuple-element.60), channel_id=1, source_target_pairs={{0,8},{1,9},{2,10},{3,11},{4,12},{5,13},{6,14},{7,15},{8,0},{9,1},... | collective-permute-start | bytes 393224 | tf_op jit(solution)/shard_map/ppermute | solution.py:487
  32.1 6.8 %all-to-all-start = ((f32[16,16,128]{2,1,0:T(8,128)}), f32[16,16,128]{2,1,0:T(8,128)S(1)}, u32[]{:S(2)}, u32[]{:S(2)}) async-start(f32[16,16,128]{2,1,0:T(8,128)} %get-tuple-element.61), calls=%async_computation | async-start | bytes 262144 | tf_op jit(solution)/shard_map/all_to_all | solution.py:489
  38.9 0.0 collective-permute-done.6.passed_ref
  38.9 0.0 copy-done.1
  38.9 5.1 %particle.1._ = f32[4,10,256,128]{3,2,1,0:T(8,128)} custom-call(s32[16]{0:T(128)S(1)} %copy-done.2, f32[4,10,256,128]{3,2,1,0:T(8,128)} %bitcast.15, f32[4,256,128]{2,1,0:T(8,128)S(1)} %bitcast.11, f32[30,16,128]{2,1,0:T(8,128)S(1)} %bitcast.8, f32[30,16,128]{2,1,0:T(8,128)S(1)} %collective-permute-done.other_ref, ...), custom_call_target="tpu_custom_call" | custom-call | flops 262144000 | bytes 10485760 | tf_op jit(solution)/shard_map/particle/pallas_call | solution.py:331
  44.0 0.0 collective-permute-done.10.refs_3_
  44.0 1.6 %all-to-all-done.faces_ref = f32[16,16,128]{2,1,0:T(8,128)S(1)} async-done(((f32[16,16,128]{2,1,0:T(8,128)}), f32[16,16,128]{2,1,0:T(8,128)S(1)}, u32[]{:S(2)}, u32[]{:S(2)}) %all-to-all-start) | async-done | bytes 131104 | tf_op jit(solution)/shard_map/all_to_all | solution.py:489
  45.6 0.0 collective-permute-done.8.refs_1_
  45.6 0.0 collective-permute-done.9.refs_2_
  45.6 0.0 collective-permute-done.7.refs_0_
  45.7 5.4 %collective-permute-start.11 = (f32[48,16,128]{2,1,0:T(8,128)S(1)}, f32[48,16,128]{2,1,0:T(8,128)S(1)}, u32[]{:S(2)}, u32[]{:S(2)}) collective-permute-start(f32[48,16,128]{2,1,0:T(8,128)S(1)} %pass_kinetic.1), channel_id=1, source_target_pairs={{0,1},{1,0},{2,3},{3,2},{4,5},{5,4},{6,7},{7,6},{8,9},{9,8},{10,11... | collective-permute-start | bytes 1179656 | tf_op jit(solution)/shard_map/ppermute | solution.py:493
  51.1 1.3 %collective-permute-done.11.passed_ref = f32[48,16,128]{2,1,0:T(8,128)S(1)} collective-permute-done((f32[48,16,128]{2,1,0:T(8,128)S(1)}, f32[48,16,128]{2,1,0:T(8,128)S(1)}, u32[]{:S(2)}, u32[]{:S(2)}) %collective-permute-start.11) | collective-permute-done | bytes 393248 | tf_op jit(solution)/shard_map/ppermute | solution.py:493
  52.4 2.2 %column.1 = f32[30,16,128]{2,1,0:T(8,128)} custom-call(s32[16]{0:T(128)S(1)} %copy-done.2, s32[2,16]{1,0:T(2,128)S(1)} %bitcast.13, f32[30,16,128]{2,1,0:T(8,128)S(1)} %bitcast.9, f32[30,16,128]{2,1,0:T(8,128)S(1)} %collective-permute-done.other_ref, f32[9,32,128]{2,1,0:T(8,128)S(1)} %collective-permute-done.1.refs_0_.edge_ref, ...), custom_call_target="tpu_custom_call" | custom-call | flops 12288000 | bytes 491520 | tf_op jit(solution)/shard_map/column/pallas_call | solution.py:449
  (1 shorter events, 0.0 us)
Async XLA Ops:
  0.6 6.6 %copy-start = (f32[1,30,16,128]{3,2,1,0:T(8,128)S(1)}, f32[1,30,16,128]{3,2,1,0:T(8,128)}, u32[]{:S(2)}) copy-start(f32[1,30,16,128]{3,2,1,0:T(8,128)} %param.6) | copy-start | bytes 737284
  0.6 38.3 %copy-start.1 = (f32[1,4,256,128]{3,2,1,0:T(8,128)S(1)}, f32[1,4,256,128]{3,2,1,0:T(8,128)}, u32[]{:S(2)}) copy-start(f32[1,4,256,128]{3,2,1,0:T(8,128)} %param.7) | copy-start | bytes 1572868
  0.7 6.6 %copy-start.2 = (s32[16]{0:T(128)S(1)}, s32[16]{0:T(128)}, u32[]{:S(2)}) copy-start(s32[16]{0:T(128)} %counts_ref.9) | copy-start | bytes 196
  0.7 6.6 %copy-start.3 = (s32[16,2]{0,1:T(2,128)S(1)}, s32[16,2]{0,1:T(2,128)}, u32[]{:S(2)}) copy-start(s32[16,2]{0,1:T(2,128)} %param.9) | copy-start | bytes 388
  0.7 4.7 %collective-permute-start = (f32[30,16,128]{2,1,0:T(8,128)}, f32[30,16,128]{2,1,0:T(8,128)S(1)}, u32[]{:S(2)}, u32[]{:S(2)}) collective-permute-start(f32[30,16,128]{2,1,0:T(8,128)} %bitcast.6), channel_id=1, source_target_pairs={{0,1},{1,0},{2,3},{3,2},{4,5},{5,4},{6,7},{7,6},{8,9},{9,8},{10,11... | collective-permute-start | bytes 737288 | tf_op jit(solution)/shard_map/ppermute | solution.py:477
  6.8 6.8 %collective-permute-start.2 = (f32[32,32,128]{2,1,0:T(8,128)S(1)}, f32[32,32,128]{2,1,0:T(8,128)S(1)}, u32[]{:S(2)}, u32[]{:S(2)}) collective-permute-start(f32[32,32,128]{2,1,0:T(8,128)S(1)} %get-tuple-element.41), channel_id=1, source_target_pairs={{0,1},{1,0},{2,3},{3,2},{4,5},{5,4},{6,7},{7,6},{8,9},{9,8},{10,11... | collective-permute-start | bytes 1572872 | tf_op jit(solution)/shard_map/ppermute | solution.py:480
  8.5 11.4 %collective-permute-start.1 = (f32[9,32,128]{2,1,0:T(8,128)S(1)}, f32[9,32,128]{2,1,0:T(8,128)S(1)}, u32[]{:S(2)}, u32[]{:S(2)}) collective-permute-start(f32[9,32,128]{2,1,0:T(8,128)S(1)} %get-tuple-element.36), channel_id=1, source_target_pairs={{0,2},{1,15},{2,4},{3,1},{4,6},{5,3},{6,8},{7,5},{8,10},{9,7},{10,... | collective-permute-start | bytes 442376 | tf_op jit(solution)/shard_map/ppermute | solution.py:484
  12.4 7.6 %collective-permute-start.3 = (f32[8,32,128]{2,1,0:T(8,128)S(1)}, f32[8,32,128]{2,1,0:T(8,128)S(1)}, u32[]{:S(2)}, u32[]{:S(2)}) collective-permute-start(f32[8,32,128]{2,1,0:T(8,128)S(1)} %get-tuple-element.48), channel_id=1, source_target_pairs={{0,4},{1,13},{2,6},{3,15},{4,8},{5,1},{6,10},{7,3},{8,12},{9,5},{1... | collective-permute-start | bytes 393224 | tf_op jit(solution)/shard_map/ppermute | solution.py:484
  15.0 7.0 %collective-permute-start.4 = (f32[8,32,128]{2,1,0:T(8,128)S(1)}, f32[8,32,128]{2,1,0:T(8,128)S(1)}, u32[]{:S(2)}, u32[]{:S(2)}) collective-permute-start(f32[8,32,128]{2,1,0:T(8,128)S(1)} %get-tuple-element.51), channel_id=1, source_target_pairs={{0,6},{1,11},{2,8},{3,13},{4,10},{5,15},{6,12},{7,1},{8,14},{9,3},... | collective-permute-start | bytes 393224 | tf_op jit(solution)/shard_map/ppermute | solution.py:484
  15.5 10.5 %collective-permute-start.5 = (f32[8,16,128]{2,1,0:T(8,128)S(1)}, f32[8,16,128]{2,1,0:T(8,128)S(1)}, u32[]{:S(2)}, u32[]{:S(2)}) collective-permute-start(f32[8,16,128]{2,1,0:T(8,128)S(1)} %get-tuple-element.54), channel_id=1, source_target_pairs={{0,8},{1,9},{2,10},{3,11},{4,12},{5,13},{6,14},{7,15},{8,0},{9,1},... | collective-permute-start | bytes 196616 | tf_op jit(solution)/shard_map/ppermute | solution.py:484
  20.0 25.6 %collective-permute-start.8 = (f32[16,32,128]{2,1,0:T(8,128)}, f32[16,32,128]{2,1,0:T(8,128)S(1)}, u32[]{:S(2)}, u32[]{:S(2)}) collective-permute-start(f32[16,32,128]{2,1,0:T(8,128)} %get-tuple-element.58), channel_id=1, source_target_pairs={{0,4},{1,13},{2,6},{3,15},{4,8},{5,1},{6,10},{7,3},{8,12},{9,5},{1... | collective-permute-start | bytes 786440 | tf_op jit(solution)/shard_map/ppermute | solution.py:487
  21.2 24.5 %collective-permute-start.9 = (f32[16,32,128]{2,1,0:T(8,128)}, f32[16,32,128]{2,1,0:T(8,128)S(1)}, u32[]{:S(2)}, u32[]{:S(2)}) collective-permute-start(f32[16,32,128]{2,1,0:T(8,128)} %get-tuple-element.59), channel_id=1, source_target_pairs={{0,6},{1,11},{2,8},{3,13},{4,10},{5,15},{6,12},{7,1},{8,14},{9,3},... | collective-permute-start | bytes 786440 | tf_op jit(solution)/shard_map/ppermute | solution.py:487
  22.1 23.6 %collective-permute-start.7 = (f32[16,32,128]{2,1,0:T(8,128)S(1)}, f32[16,32,128]{2,1,0:T(8,128)S(1)}, u32[]{:S(2)}, u32[]{:S(2)}) collective-permute-start(f32[16,32,128]{2,1,0:T(8,128)S(1)} %get-tuple-element.57), channel_id=1, source_target_pairs={{0,2},{1,15},{2,4},{3,1},{4,6},{5,3},{6,8},{7,5},{8,10},{9,7},{10,... | collective-permute-start | bytes 786440 | tf_op jit(solution)/shard_map/ppermute | solution.py:487
  26.6 12.3 %collective-permute-start.6 = (f32[14,32,128]{2,1,0:T(8,128)S(1)}, f32[14,32,128]{2,1,0:T(8,128)S(1)}, u32[]{:S(2)}, u32[]{:S(2)}) collective-permute-start(f32[14,32,128]{2,1,0:T(8,128)S(1)} %pass_rise.1), channel_id=1, source_target_pairs={{0,1},{1,0},{2,3},{3,2},{4,5},{5,4},{6,7},{7,6},{8,9},{9,8},{10,11... | collective-permute-start | bytes 688136 | tf_op jit(solution)/shard_map/ppermute | solution.py:490
  28.8 15.2 %collective-permute-start.10 = (f32[16,16,128]{2,1,0:T(8,128)S(1)}, f32[16,16,128]{2,1,0:T(8,128)S(1)}, u32[]{:S(2)}, u32[]{:S(2)}) collective-permute-start(f32[16,16,128]{2,1,0:T(8,128)S(1)} %get-tuple-element.60), channel_id=1, source_target_pairs={{0,8},{1,9},{2,10},{3,11},{4,12},{5,13},{6,14},{7,15},{8,0},{9,1},... | collective-permute-start | bytes 393224 | tf_op jit(solution)/shard_map/ppermute | solution.py:487
  32.1 13.5 %all-to-all-start = ((f32[16,16,128]{2,1,0:T(8,128)}), f32[16,16,128]{2,1,0:T(8,128)S(1)}, u32[]{:S(2)}, u32[]{:S(2)}) async-start(f32[16,16,128]{2,1,0:T(8,128)} %get-tuple-element.61), calls=%async_computation | async-start | bytes 262144 | tf_op jit(solution)/shard_map/all_to_all | solution.py:489
  45.7 6.7 %collective-permute-start.11 = (f32[48,16,128]{2,1,0:T(8,128)S(1)}, f32[48,16,128]{2,1,0:T(8,128)S(1)}, u32[]{:S(2)}, u32[]{:S(2)}) collective-permute-start(f32[48,16,128]{2,1,0:T(8,128)S(1)} %pass_kinetic.1), channel_id=1, source_target_pairs={{0,1},{1,0},{2,3},{3,2},{4,5},{5,4},{6,7},{7,6},{8,9},{9,8},{10,11... | collective-permute-start | bytes 1179656 | tf_op jit(solution)/shard_map/ppermute | solution.py:493
